TPU v7x, 32 devices: a whole 2x2x4 slice. The times are simulated.
32 devices in a mesh: groups: 2 (over x), bus: 16 (over z, y, core).
Axes of the slice: x: 2, y: 2, z: 4, core: 2. Of those that a mesh axis runs over, the one named last changes fastest.
Arguments:
- generation: float32 [512, 32], P('bus', 'groups'), parts along dimension 1, may hold values from 0 to 1
- charging: float32 [32, 512], P('groups', 'bus'), parts along dimension 0, may hold values from -1.5 to 1.5
- flow_dual: float32 [4096, 32], P('bus', 'groups'), parts along dimension 1, may hold values from -3 to 3
- energy_dual: float32 [32, 512], P('groups', 'bus'), parts along dimension 0, may hold values from -1.6 to 1.6
- shift_factors: float32 [4096, 16384], P(None, 'bus'), may hold values from -0.0625 to 0.0625
- load_units: int32 [16384, 32], P('bus', 'groups'), parts along dimension 1, may hold values from 0 to 59
- generator_bus: int32 [512], P('bus'), may hold values from 0 to 16383, as said below
- storage_bus: int32 [512], P('bus'), may hold values from 0 to 16383, as said below
- generator_cost: float32 [512], P('bus'), may hold values from 0.05 to 0.5
- generator_max: float32 [512], P('bus'), may hold values from 1 to 4
- charging_max: float32 [512], replicated, may hold values from 2 to 4
- energy_init: float32 [512], replicated, may hold values from 0.5 to 2
- energy_max: float32 [512], replicated, may hold values from 2.5 to 4
- line_max: float32 [4096], P('bus'), may hold values from 0.5 to 3
Outputs:
- generation_new: float32 [512, 32], P('bus', 'groups'), parts along dimension 1
- charging_new: float32 [32, 512], P('groups', 'bus'), parts along dimension 0
- flow_dual_new: float32 [4096, 32], P('bus', 'groups'), parts along dimension 1
- energy_dual_new: float32 [32, 512], P('groups', 'bus'), parts along dimension 0
There are 2 independent parts, one for each index of `groups`. A program takes and returns all parts, laid end to end along the dimension named above; an argument that names none is the same for every part. Nothing has to cross between parts.
Inputs may be any that keep to these rules, and one draw needn't show every extreme that they name: `generator_bus`: generator g sits at one of the buses g // 32 * 1024 to (g // 32 + 1) * 1024 - 1. `storage_bus`: storage unit k sits at one of the buses k // 32 * 1024 to (k // 32 + 1) * 1024 - 1.
All inputs are finite; a program needn't handle non-finite values.
Results may differ from a plain program's by a relative error of at most 0.00023.
Values sent between devices are 32-bit elements; how exact they have to be, the bound alone decides.
A program may use at most 64 MiB of HBM per device.

v0:
```python
import jax
import jax.numpy as jnp
from jax import lax
from jax.sharding import PartitionSpec as P

ITERS = 3


primal_step = 0.5
dual_step = 0.5
energy_step = 0.05
efficiency = 0.95
interval = 0.125
load_unit = 0.05
highest = lax.Precision.HIGHEST
across_first = (((0,), (0,)), ((), ()))
across_second = (((1,), (1,)), ((), ()))
inner_pair = (((1,), (0,)), ((), ()))


def contract(left, right, dims):
    return lax.dot_general(left, right, dims, precision=highest, preferred_element_type=jnp.float32)


def reverse_cumsum(values):
    return jnp.flip(jnp.cumsum(jnp.flip(values, 0), axis=0), 0)


def clip_dual(shifted, step_size, low_bound, high_bound):
    return shifted - step_size * jnp.clip(shifted / step_size, low_bound, high_bound)


def on_device(
    generation,
    charging,
    flow_dual,
    energy_dual,
    shift_factors,
    load_units,
    generator_bus,
    storage_bus,
    generator_cost,
    generator_max,
    charging_max,
    energy_init,
    energy_max,
    line_max,
):
    bus_local = shift_factors.shape[1]
    stor_local = storage_bus.shape[0]
    own_index = lax.axis_index("bus")
    bus_ids = lax.broadcasted_iota(jnp.int32, (bus_local, 1), 0) + own_index * bus_local
    gen_onehot = (generator_bus[None, :] == bus_ids).astype(jnp.float32)
    stor_onehot = (storage_bus[None, :] == bus_ids).astype(jnp.float32)
    demand = load_units.astype(jnp.float32) * load_unit
    unit_cost = generator_cost[:, None]
    ceiling = generator_max[:, None]
    first_slot = own_index * stor_local
    charge_limit = lax.dynamic_slice_in_dim(charging_max, first_slot, stor_local)[None, :]
    start_energy = lax.dynamic_slice_in_dim(energy_init, first_slot, stor_local)[None, :]
    energy_limit = lax.dynamic_slice_in_dim(energy_max, first_slot, stor_local)[None, :]
    for iteration in range(ITERS):
        prices = contract(
            shift_factors, lax.all_gather(flow_dual, "bus", axis=0, tiled=True), across_first
        )
        gen_step = jnp.clip(
            generation - primal_step * (unit_cost + contract(gen_onehot, prices, across_first)),
            0.0,
            ceiling,
        )
        gen_bar = 2.0 * gen_step - generation
        stor_prices = contract(prices, stor_onehot, across_first)
        gradient = efficiency * interval * reverse_cumsum(energy_dual) - stor_prices
        charge_step = jnp.clip(charging - primal_step * gradient, -charge_limit, charge_limit)
        bar_bus = 2.0 * charge_step - charging
        energy = start_energy + efficiency * interval * jnp.cumsum(bar_bus, axis=0)
        energy_dual = clip_dual(energy_dual + energy_step * energy, energy_step, 0.0, energy_limit)
        charging = charge_step
        injected = (
            contract(gen_onehot, gen_bar, inner_pair)
            - contract(stor_onehot, bar_bus, across_second)
            - demand
        )
        line_flows = lax.psum_scatter(
            contract(shift_factors, injected, inner_pair), "bus", scatter_dimension=0, tiled=True
        )
        flow_dual = clip_dual(
            flow_dual + dual_step * line_flows, dual_step, -line_max[:, None], line_max[:, None]
        )
        generation = gen_step
    return (generation, charging, flow_dual, energy_dual)


def solution(mesh):
    placed = (
        P("bus", "groups"),
        P("groups", "bus"),
        P("bus", "groups"),
        P("groups", "bus"),
        P(None, "bus"),
        P("bus", "groups"),
        P("bus"),
        P("bus"),
        P("bus"),
        P("bus"),
        P(),
        P(),
        P(),
        P("bus"),
    )
    return jax.shard_map(
        on_device,
        mesh=mesh,
        in_specs=placed,
        out_specs=(P("bus", "groups"), P("groups", "bus"), P("bus", "groups"), P("groups", "bus")),
        check_vma=False,
    )
```

profile of v0, /device:TPU:0, one launch (start us, length us, event | category | flops | bytes accessed | tf_op | source)
XLA Modules:
  0.0 333.9 jit_solution(3252353573156793211)
XLA Ops:
  7.3 0.7 rev.19
  8.0 24.0 %all_gather.9 = f32[4096,16]{0,1:T(8,128)S(1)} all-gather(f32[256,16]{0,1:T(8,128)} %param.16), channel_id=1, replica_groups=mesh['groups'=2,'bus'=16] {'bus'}, dimensions={0}, use_global_device_ids=true | all-gather | bytes 278528 | tf_op jit(solution)/shard_map/all_gather | solution.py:64
  32.1 0.9 fusion.168
  33.0 12.9 %fusion.169 = f32[1024,16]{0,1:T(8,128)S(1)} fusion(f32[4096,1024]{1,0:T(8,128)} %param.18, f32[4096,16]{0,1:T(8,128)S(1)} %all_gather.9), kind=kOutput, calls=%fused_computation.111 | convolution fusion | flops 805306368 | bytes 17104896 | tf_op jit(solution)/shard_map/dot_general | solution.py:22
  46.0 0.4 multiply_subtract_fusion.8
  46.4 0.5 fusion.8
  46.9 0.4 fusion.54
  47.3 0.5 fusion.27
  47.7 14.9 %convolution_bitcast_fusion.2 = f32[4096,16]{0,1:T(8,128)} fusion(f32[1024,16]{0,1:T(8,128)S(1)} %fusion.27, f32[4096,1024]{1,0:T(8,128)S(1)} %copy-done), kind=kOutput, calls=%fused_computation.2 | convolution fusion | flops 805306368 | bytes 17104896 | tf_op jit(solution)/shard_map/dot_general | solution.py:22
  62.7 0.8 dynamic_slice.10
  63.5 0.8 dynamic_slice.11
  64.3 51.1 %reduce-scatter.4.cloned.1.call-done = f32[256,16]{0,1:T(8,128)} async-done(((f32[4096,16]{0,1:T(8,128)}), f32[256,16]{0,1:T(8,128)}) %reduce-scatter.4.cloned.1.call-update) | async-done | bytes 16400 | tf_op jit(solution)/shard_map/reduce_scatter | solution.py:84
  115.4 0.7 multiply_subtract_fusion.2
  116.1 20.1 %all_gather.10 = f32[4096,16]{0,1:T(8,128)S(1)} all-gather(f32[256,16]{0,1:T(8,128)S(1)} %multiply_subtract_fusion.2), channel_id=1, replica_groups=mesh['groups'=2,'bus'=16] {'bus'}, dimensions={0}, use_global_device_ids=true | all-gather | bytes 278528 | tf_op jit(solution)/shard_map/all_gather | solution.py:64
  136.3 11.6 %fusion.170 = f32[16,1024]{1,0:T(8,128)S(1)} fusion(f32[4096,16]{0,1:T(8,128)S(1)} %all_gather.10, f32[4096,1024]{1,0:T(8,128)} %param.18), kind=kOutput, calls=%fused_computation.112 | convolution fusion | flops 805306368 | bytes 17104896 | tf_op jit(solution)/shard_map/dot_general | solution.py:22
  147.8 0.4 fusion.69
  148.2 0.4 multiply_subtract_fusion.6
  148.6 0.5 fusion.4
  149.1 0.5 fusion.33
  149.5 17.8 %convolution_bitcast_fusion.1 = f32[4096,16]{0,1:T(8,128)} fusion(f32[1024,16]{0,1:T(8,128)S(1)} %fusion.33, f32[4096,1024]{1,0:T(8,128)} %param.18), kind=kOutput, calls=%fused_computation.1 | convolution fusion | flops 805306368 | bytes 17104896 | tf_op jit(solution)/shard_map/dot_general | solution.py:22
  167.5 52.5 %reduce-scatter.6.cloned.1.call-done = f32[256,16]{0,1:T(8,128)} async-done(((f32[4096,16]{0,1:T(8,128)}), f32[256,16]{0,1:T(8,128)}) %reduce-scatter.6.cloned.1.call-update) | async-done | bytes 16400 | tf_op jit(solution)/shard_map/reduce_scatter | solution.py:84
  220.0 0.7 multiply_subtract_fusion.1
  220.7 20.2 %all_gather.11 = f32[4096,16]{0,1:T(8,128)S(1)} all-gather(f32[256,16]{0,1:T(8,128)S(1)} %multiply_subtract_fusion.1), channel_id=1, replica_groups=mesh['groups'=2,'bus'=16] {'bus'}, dimensions={0}, use_global_device_ids=true | all-gather | bytes 278528 | tf_op jit(solution)/shard_map/all_gather | solution.py:64
  240.9 11.8 %fusion.171 = f32[16,1024]{1,0:T(8,128)S(1)} fusion(f32[4096,16]{0,1:T(8,128)S(1)} %all_gather.11, f32[4096,1024]{1,0:T(8,128)} %param.18), kind=kOutput, calls=%fused_computation.113 | convolution fusion | flops 805306368 | bytes 17104896 | tf_op jit(solution)/shard_map/dot_general | solution.py:22
  252.7 0.4 fusion.84
  253.1 1.0 multiply_subtract_fusion.4
  254.1 0.4 fusion
  254.5 0.5 fusion.39
  255.0 17.8 %convolution_bitcast_fusion = f32[4096,16]{0,1:T(8,128)} fusion(f32[1024,16]{0,1:T(8,128)S(1)} %fusion.39, f32[4096,1024]{1,0:T(8,128)} %param.18), kind=kOutput, calls=%fused_computation | convolution fusion | flops 805306368 | bytes 17104896 | tf_op jit(solution)/shard_map/dot_general | solution.py:22
  272.9 0.6 multiply_subtract_fusion.3
  273.5 52.1 %reduce-scatter.8.cloned.1.call-done = f32[256,16]{0,1:T(8,128)} async-done(((f32[4096,16]{0,1:T(8,128)}), f32[256,16]{0,1:T(8,128)}) %reduce-scatter.8.cloned.1.call-update) | async-done | bytes 16400 | tf_op jit(solution)/shard_map/reduce_scatter | solution.py:84
  325.6 1.3 multiply_subtract_fusion
  (45 shorter events, 0.5 us)
Async XLA Ops:
  7.2 38.8 %copy-start.11 = (s32[32]{0:T(128)S(1)}, s32[32]{0:T(128)}, u32[]{:S(2)}) copy-start(s32[32]{0:T(128)} %param.21) | copy-start | bytes 388
  7.2 38.8 %copy-start.8 = (f32[16,32]{1,0:T(8,128)S(1)}, f32[16,32]{1,0:T(8,128)}, u32[]{:S(2)}) copy-start(f32[16,32]{1,0:T(8,128)} %param.15) | copy-start | bytes 6148
  7.2 39.6 %copy-start.7 = (s32[32]{0:T(128)S(1)}, s32[32]{0:T(128)}, u32[]{:S(2)}) copy-start(s32[32]{0:T(128)} %param.20) | copy-start | bytes 388
  7.2 39.6 %copy-start.10 = (f32[32]{0:T(128)S(1)}, f32[32]{0:T(128)}, u32[]{:S(2)}) copy-start(f32[32]{0:T(128)} %param.23) | copy-start | bytes 388
  7.2 39.6 %copy-start.9 = (f32[32]{0:T(128)S(1)}, f32[32]{0:T(128)}, u32[]{:S(2)}) copy-start(f32[32]{0:T(128)} %param.22) | copy-start | bytes 388
  7.2 39.6 %copy-start.5 = (f32[32,16]{0,1:T(8,128)S(1)}, f32[32,16]{0,1:T(8,128)}, u32[]{:S(2)}) copy-start(f32[32,16]{0,1:T(8,128)} %param.14) | copy-start | bytes 6148
  7.2 40.0 %copy-start.1 = (s32[1024,16]{0,1:T(8,128)S(1)}, s32[1024,16]{0,1:T(8,128)}, u32[]{:S(2)}) copy-start(s32[1024,16]{0,1:T(8,128)} %param.19) | copy-start | bytes 196612
  7.2 108.2 %reduce-scatter.4.cloned.1.call-start = ((), (), s32[]{:S(2)}) async-start(), calls=%async_computation.3 | async-start | bytes 278528 | tf_op jit(solution)/shard_map/reduce_scatter | solution.py:84
  32.1 15.6 %copy-start = (f32[4096,1024]{1,0:T(8,128)S(1)}, f32[4096,1024]{1,0:T(8,128)}, u32[]{:S(2)}) copy-start(f32[4096,1024]{1,0:T(8,128)} %param.18) | copy-start | bytes 50331652
  33.0 31.2 %copy-start.4 = (f32[256]{0:T(256)S(1)}, f32[256]{0:T(256)}, u32[]{:S(2)}) copy-start(f32[256]{0:T(256)} %param.27) | copy-start | bytes 3076
  33.0 31.2 %copy-start.3 = (f32[16,32]{1,0:T(8,128)S(1)}, f32[16,32]{1,0:T(8,128)}, u32[]{:S(2)}) copy-start(f32[16,32]{1,0:T(8,128)} %param.17) | copy-start | bytes 6148
  33.0 82.4 %copy-start.2 = (f32[256,16]{0,1:T(8,128)S(1)}, f32[256,16]{0,1:T(8,128)}, u32[]{:S(2)}) copy-start(f32[256,16]{0,1:T(8,128)} %param.16) | copy-start | bytes 49156
  62.6 157.4 %reduce-scatter.6.cloned.1.call-start = ((), (), s32[]{:S(2)}) async-start(), calls=%async_computation.4 | async-start | bytes 278528 | tf_op jit(solution)/shard_map/reduce_scatter | solution.py:84
  167.3 158.2 %reduce-scatter.8.cloned.1.call-start = ((), (), s32[]{:S(2)}) async-start(), calls=%async_computation.5 | async-start | bytes 278528 | tf_op jit(solution)/shard_map/reduce_scatter | solution.py:84
  253.1 73.8 %copy-start.6 = (f32[32,16]{0,1:T(8,128)}, f32[32,16]{0,1:T(8,128)S(1)}, u32[]{:S(2)}) copy-start(f32[32,16]{0,1:T(8,128)S(1)} %fusion.84) | copy-start | bytes 6148
Sparse Core Ops, SparseCore 0:
  62.7 52.6 reduce-scatter.3
  167.5 52.5 reduce-scatter.5
  273.0 52.5 reduce-scatter.7
where the time goes:
time: 338 us; the launch traced here: 334 us
  waiting for transfers between devices  156 us (46%)
  matrix products  92.4 us (27%)
  blocking collectives  64.3 us (19%)
  between operations  14.4 us (4%)
  other arithmetic  4.55 us (1%)
    reduce_scatter x3, waiting for transfers between devices, on_device(): lax.psum_scatter(contract(shift_factors, injected, inner_pair), 'bus', sc...  156 us
    dot_general x18, matrix products, contract(): lax.dot_general(left, right, dims, precision=highest, preferred_element_t...  92.4 us
    all_gather x3, blocking collectives, on_device(): lax.all_gather(flow_dual, 'bus', axis=0, tiled=True)  64.3 us
  transfers between devices with their start and end apart: 3, of which 3 were waited for; matrix products, arithmetic and copies ran while one was open for 1% of the time, Pallas kernels for 0%

commit v1 on v0

v1 whole, which is shorter than its diff:
```python
import functools

import jax
import jax.numpy as jnp
from jax import lax
from jax.experimental import pallas as pl
from jax.experimental.pallas import tpu as pltpu
from jax.sharding import PartitionSpec as P

ITERS = 3
LANES = 128
MESH = pl.DeviceIdType.MESH

primal_step = 0.5
dual_step = 0.5
energy_step = 0.05
efficiency = 0.95
interval = 0.125
load_unit = 0.05
highest = lax.Precision.HIGHEST
across_first = (((0,), (0,)), ((), ()))
across_second = (((1,), (1,)), ((), ()))
inner_pair = (((1,), (0,)), ((), ()))


def contract(left, right, dims):
    return lax.dot_general(left, right, dims, precision=highest, preferred_element_type=jnp.float32)


def reverse_cumsum(values):
    return jnp.flip(jnp.cumsum(jnp.flip(values, 0), axis=0), 0)


def clip_dual(shifted, step_size, low_bound, high_bound):
    return shifted - step_size * jnp.clip(shifted / step_size, low_bound, high_bound)


def split_bf16(values):
    high = values.astype(jnp.bfloat16)
    return high, (values - high.astype(jnp.float32)).astype(jnp.bfloat16)


def running_sum(values, backward):
    rows = values.shape[0]
    row = lax.broadcasted_iota(jnp.int32, values.shape, 0)
    step = 1
    while step < rows:
        if backward:
            moved = jnp.where(row < rows - step, pltpu.roll(values, rows - step, 0), 0.0)
        else:
            moved = jnp.where(row >= step, pltpu.roll(values, step, 0), 0.0)
        values = values + moved
        step *= 2
    return values


def iterate_kernel(
    n_bus,
    gen_ref,
    charge_ref,
    dual_ref,
    energy_ref,
    factors_ref,
    load_ref,
    gen_bus_ref,
    stor_bus_ref,
    cost_ref,
    gen_max_ref,
    charge_max_ref,
    init_ref,
    energy_max_ref,
    line_max_ref,
    gen_out,
    charge_out,
    dual_out,
    energy_out,
    factors_buf,
    place_buf,
    pack_own,
    pack_sib,
    cols_send,
    cols_recv,
    weight_buf,
    demand_buf,
    dual_buf,
    flow_send,
    flow_recv,
    price_send,
    price_recv,
    factors_sem,
    pack_sem,
    cols_sems,
    dual_send_sem,
    dual_recv_sem,
    flow_send_sem,
    flow_recv_sem,
    price_sem,
):
    chips = n_bus // 2
    hours, units = gen_ref.shape
    block = dual_ref.shape[1]
    buses = factors_ref.shape[1]
    half = 2 * units
    width = 2 * half
    me = lax.axis_index("bus")
    core = lax.rem(me, 2)
    chip = lax.div(me, 2)
    sibling = me + 1 - 2 * core

    def peer(k):
        return lax.rem(chip + k, chips)

    def load_factors(i, parity):
        b = 2 * i + parity
        start = pl.multiple_of(b * block, block)
        return pltpu.make_async_copy(
            factors_ref.at[pl.ds(start, block), :], factors_buf.at[b], factors_sem.at[b]
        )

    @pl.loop(0, chips)
    def _(i):
        load_factors(i, 1 - core).start()

    @pl.loop(0, chips)
    def _(i):
        load_factors(i, core).start()

    barrier = pltpu.get_barrier_semaphore()
    for k in range(1, chips):
        pl.semaphore_signal(
            barrier, inc=1, device_id={"bus": 2 * peer(k) + core}, device_id_type=MESH
        )
    pl.semaphore_signal(barrier, inc=1, device_id={"bus": sibling}, device_id_type=MESH)
    pl.semaphore_wait(barrier, chips)

    def send_dual(t, k):
        source = dual_ref if t == 0 else dual_buf.at[t, chip]
        return pltpu.make_async_remote_copy(
            src_ref=source,
            dst_ref=dual_buf.at[t, chip],
            send_sem=dual_send_sem.at[t, k],
            recv_sem=dual_recv_sem.at[t, chip],
            device_id={"bus": 2 * peer(k) + core},
            device_id_type=MESH,
        )

    def recv_dual(t, c):
        return pltpu.make_async_remote_copy(
            src_ref=dual_buf.at[t, c],
            dst_ref=dual_buf.at[t, c],
            send_sem=dual_send_sem.at[t, 0],
            recv_sem=dual_recv_sem.at[t, c],
            device_id={"bus": sibling},
            device_id_type=MESH,
        )

    def send_flow(t, k):
        return pltpu.make_async_remote_copy(
            src_ref=flow_send.at[t, k],
            dst_ref=flow_recv.at[t, chip],
            send_sem=flow_send_sem.at[t, k],
            recv_sem=flow_recv_sem.at[t, chip],
            device_id={"bus": 2 * peer(k) + core},
            device_id_type=MESH,
        )

    def recv_flow(t, c):
        return pltpu.make_async_remote_copy(
            src_ref=flow_recv.at[t, c],
            dst_ref=flow_recv.at[t, c],
            send_sem=flow_send_sem.at[t, 0],
            recv_sem=flow_recv_sem.at[t, c],
            device_id={"bus": sibling},
            device_id_type=MESH,
        )

    def to_sibling(source, target, sems):
        return pltpu.make_async_remote_copy(
            src_ref=source,
            dst_ref=target,
            send_sem=sems.at[0],
            recv_sem=sems.at[1],
            device_id={"bus": sibling},
            device_id_type=MESH,
        )

    for k in range(1, chips):
        send_dual(0, k).start()

    gens = slice(0, units)
    stors = slice(units, half)
    pack_own[...] = jnp.zeros_like(pack_own)
    pack_own[0, :, gens] = gen_ref[...]
    pack_own[0, :, stors] = charge_ref[...]
    pack_own[1, :, stors] = energy_ref[...]
    pack_own[2, 0:1, gens] = cost_ref[...]
    pack_own[2, 1:2, gens] = gen_max_ref[...]
    first = me * units
    lane_start = pl.multiple_of(lax.div(first, LANES) * LANES, LANES)
    shift = lax.rem(units - lax.rem(first, LANES) + LANES, LANES)
    for row, ref in ((1, charge_max_ref), (2, init_ref), (3, energy_max_ref)):
        chunk = jnp.broadcast_to(ref[0:1, pl.ds(lane_start, LANES)], (8, LANES))
        pack_own[2, row : row + 1, stors] = pltpu.roll(chunk, shift, 1)[0:1, stors]
    send_pack = to_sibling(pack_own, pack_sib, pack_sem)
    send_pack.start()

    pack_index = jnp.full((8, LANES), -1, jnp.int32)
    lane8 = lax.broadcasted_iota(jnp.int32, (8, LANES), 1)
    for at, ref in ((0, gen_bus_ref), (units, stor_bus_ref)):
        padded = jnp.concatenate([ref[...], jnp.zeros((1, LANES - units), jnp.int32)], axis=1)
        padded = pltpu.roll(jnp.broadcast_to(padded, (8, LANES)), at, 1)
        pack_index = jnp.where((lane8 >= at) & (lane8 < at + units), padded - me * buses, pack_index)
    bus_id = lax.broadcasted_iota(jnp.int32, (buses, LANES), 0)
    onehot = jnp.where(bus_id == pack_index[0:1, :], 1.0, 0.0)
    loads = jnp.concatenate(
        [
            jnp.zeros((half, buses), jnp.float32),
            load_ref[...].astype(jnp.float32),
            jnp.zeros((LANES - half - hours, buses), jnp.float32),
        ],
        axis=0,
    )
    place_buf[...] = (onehot + loads.T).astype(jnp.bfloat16)

    def take_columns(b):
        high, low = split_bf16(factors_buf[b])
        place = place_buf[...]
        taken = jnp.dot(high, place, preferred_element_type=jnp.float32) + jnp.dot(
            low, place, preferred_element_type=jnp.float32
        )
        return taken.T[: half + hours]

    def swap_columns(i):
        return pltpu.make_async_remote_copy(
            src_ref=cols_send.at[i],
            dst_ref=cols_recv.at[i],
            send_sem=cols_sems.at[0, i],
            recv_sem=cols_sems.at[1, i],
            device_id={"bus": sibling},
            device_id_type=MESH,
        )

    @pl.loop(0, chips)
    def _(i):
        load_factors(i, 1 - core).wait()
        cols_send[i] = take_columns(2 * i + 1 - core)
        swap_columns(i).start()

    @pl.loop(0, chips)
    def _(i):
        load_factors(i, core).wait()
        mine = take_columns(2 * i + core)
        swap_columns(i).wait()
        other = cols_recv[i]
        high, low = split_bf16(jnp.concatenate([mine[:half], other[:half]], axis=0))
        weight_buf[i, 0:width] = high
        weight_buf[i, width : 2 * width] = low
        demand_buf[i] = load_unit * (mine[half:] + other[half:])

    send_pack.wait()
    state = pack_own[0] + pltpu.roll(pack_sib[0], half, 1)
    energy_dual = pack_own[1] + pltpu.roll(pack_sib[1], half, 1)
    params = pack_own[2] + pltpu.roll(pack_sib[2], half, 1)
    cost, upper, start_energy, energy_limit = (params[r : r + 1] for r in range(4))
    lane = lax.broadcasted_iota(jnp.int32, (hours, width), 1)
    is_gen = lax.rem(lane, half) < units
    lower = jnp.where(is_gen, 0.0, -upper)
    later = running_sum(energy_dual, True)
    own_dual = dual_ref[...]
    line_max = line_max_ref[...]

    for t in range(ITERS):
        total = jnp.zeros((2 * hours, 2 * width), jnp.float32)
        for k in range(chips):
            c = peer(chips - k)
            if k == 0:
                dual = own_dual
            else:
                recv_dual(t, c).wait_recv()
                dual = dual_buf[t, c]
            pieces = jnp.concatenate(split_bf16(dual), axis=0)
            total = total + lax.dot_general(
                pieces, weight_buf[c], across_second, preferred_element_type=jnp.float32
            )
        total = total[:hours] + total[hours:]
        part = total[:, :width] + total[:, width:]
        price_send[t] = part
        swap_prices = to_sibling(price_send.at[t], price_recv.at[t], price_sem.at[t])
        swap_prices.start()
        swap_prices.wait()
        prices = part + pltpu.roll(price_recv[t], half, 1)

        gradient = jnp.where(is_gen, cost + prices, efficiency * interval * later - prices)
        step = jnp.clip(state - primal_step * gradient, lower, upper)
        bar = 2.0 * step - state
        state = step
        high, low = split_bf16(jnp.where(is_gen, bar, -bar))
        pieces = jnp.concatenate(
            [jnp.concatenate([high, high], axis=1), jnp.concatenate([low, low], axis=1)], axis=0
        )

        def flows(c):
            out = jnp.dot(pieces, weight_buf[c], preferred_element_type=jnp.float32)
            return out[:hours] + out[hours:] - demand_buf[c]

        for k in range(1, chips):
            flow_send[t, k] = flows(peer(k))
            send_flow(t, k).start()
        line_flows = flows(chip)
        energy = start_energy + efficiency * interval * running_sum(bar, False)
        energy_dual = clip_dual(energy_dual + energy_step * energy, energy_step, 0.0, energy_limit)
        if t + 1 < ITERS:
            later = running_sum(energy_dual, True)
        for k in range(1, chips):
            c = peer(chips - k)
            recv_flow(t, c).wait_recv()
            line_flows = line_flows + flow_recv[t, c]
        own_dual = clip_dual(own_dual + dual_step * line_flows, dual_step, -line_max, line_max)
        if t + 1 < ITERS:
            dual_buf[t + 1, chip] = own_dual
            for k in range(1, chips):
                send_dual(t + 1, k).start()

    dual_out[...] = own_dual
    gen_out[...] = state[:, gens]
    charge_out[...] = state[:, stors]
    energy_out[...] = energy_dual[:, stors]
    for t in range(ITERS):
        for k in range(1, chips):
            send_dual(t, k).wait_send()
            send_flow(t, k).wait_send()


def on_device_kernel(
    generation,
    charging,
    flow_dual,
    energy_dual,
    shift_factors,
    load_units,
    generator_bus,
    storage_bus,
    generator_cost,
    generator_max,
    charging_max,
    energy_init,
    energy_max,
    line_max,
):
    lines, buses = shift_factors.shape
    units, hours = generation.shape
    block = flow_dual.shape[0]
    n_bus = lines // block
    chips = n_bus // 2
    half = 2 * units
    width = 2 * half
    vmem = pl.BlockSpec(memory_space=pltpu.VMEM)
    in_specs = [vmem] * 14
    in_specs[4] = pl.BlockSpec(memory_space=pltpu.HBM)
    f32 = jnp.float32
    dma = pltpu.SemaphoreType.DMA
    gen_new, charge_new, dual_new, energy_new = pl.pallas_call(
        functools.partial(iterate_kernel, n_bus),
        out_shape=(
            jax.ShapeDtypeStruct((hours, units), f32),
            jax.ShapeDtypeStruct((hours, units), f32),
            jax.ShapeDtypeStruct((hours, block), f32),
            jax.ShapeDtypeStruct((hours, units), f32),
        ),
        in_specs=in_specs,
        out_specs=(vmem,) * 4,
        scratch_shapes=[
            pltpu.VMEM((n_bus, block, buses), f32),
            pltpu.VMEM((buses, LANES), jnp.bfloat16),
            pltpu.VMEM((3, hours, width), f32),
            pltpu.VMEM((3, hours, width), f32),
            pltpu.VMEM((chips, half + hours, block), f32),
            pltpu.VMEM((chips, half + hours, block), f32),
            pltpu.VMEM((chips, 2 * width, block), jnp.bfloat16),
            pltpu.VMEM((chips, hours, block), f32),
            pltpu.VMEM((ITERS, chips, hours, block), f32),
            pltpu.VMEM((ITERS, chips, hours, block), f32),
            pltpu.VMEM((ITERS, chips, hours, block), f32),
            pltpu.VMEM((ITERS, hours, width), f32),
            pltpu.VMEM((ITERS, hours, width), f32),
            dma((n_bus,)),
            dma((2,)),
            dma((2, chips)),
            dma((ITERS, chips)),
            dma((ITERS, chips)),
            dma((ITERS, chips)),
            dma((ITERS, chips)),
            dma((ITERS, 2)),
        ],
        compiler_params=pltpu.CompilerParams(
            collective_id=0, has_side_effects=True, vmem_limit_bytes=52 * 1024 * 1024
        ),
    )(
        generation.T,
        charging,
        flow_dual.T,
        energy_dual,
        shift_factors,
        load_units.T,
        generator_bus[None, :],
        storage_bus[None, :],
        generator_cost[None, :],
        generator_max[None, :],
        charging_max[None, :],
        energy_init[None, :],
        energy_max[None, :],
        line_max[None, :],
    )
    return gen_new.T, charge_new, dual_new.T, energy_new


def on_device(
    generation,
    charging,
    flow_dual,
    energy_dual,
    shift_factors,
    load_units,
    generator_bus,
    storage_bus,
    generator_cost,
    generator_max,
    charging_max,
    energy_init,
    energy_max,
    line_max,
):
    bus_local = shift_factors.shape[1]
    gen_local = generator_bus.shape[0]
    stor_local = storage_bus.shape[0]
    own_index = lax.axis_index("bus")
    bus_ids = lax.broadcasted_iota(jnp.int32, (bus_local, 1), 0) + own_index * bus_local
    gen_onehot = (generator_bus[None, :] == bus_ids).astype(jnp.float32)
    stor_onehot = (storage_bus[None, :] == bus_ids).astype(jnp.float32)
    columns = contract(shift_factors, jnp.concatenate([gen_onehot, stor_onehot], axis=1), inner_pair)
    demand = load_units.astype(jnp.float32) * load_unit
    demand_flows = contract(shift_factors, demand, inner_pair)
    unit_cost = generator_cost[:, None]
    ceiling = generator_max[:, None]
    first_slot = own_index * stor_local
    charge_limit = lax.dynamic_slice_in_dim(charging_max, first_slot, stor_local)[None, :]
    start_energy = lax.dynamic_slice_in_dim(energy_init, first_slot, stor_local)[None, :]
    energy_limit = lax.dynamic_slice_in_dim(energy_max, first_slot, stor_local)[None, :]
    for iteration in range(ITERS):
        prices = contract(columns, lax.all_gather(flow_dual, "bus", axis=0, tiled=True), across_first)
        gen_step = jnp.clip(
            generation - primal_step * (unit_cost + prices[:gen_local]), 0.0, ceiling
        )
        gen_bar = 2.0 * gen_step - generation
        stor_prices = prices[gen_local:].T
        gradient = efficiency * interval * reverse_cumsum(energy_dual) - stor_prices
        charge_step = jnp.clip(charging - primal_step * gradient, -charge_limit, charge_limit)
        bar_bus = 2.0 * charge_step - charging
        energy = start_energy + efficiency * interval * jnp.cumsum(bar_bus, axis=0)
        energy_dual = clip_dual(energy_dual + energy_step * energy, energy_step, 0.0, energy_limit)
        charging = charge_step
        bars = jnp.concatenate([gen_bar, -bar_bus.T], axis=0)
        line_flows = lax.psum_scatter(
            contract(columns, bars, inner_pair) - demand_flows, "bus", scatter_dimension=0, tiled=True
        )
        flow_dual = clip_dual(
            flow_dual + dual_step * line_flows, dual_step, -line_max[:, None], line_max[:, None]
        )
        generation = gen_step
    return (generation, charging, flow_dual, energy_dual)


def fits_kernel(n_bus, generation, charging, flow_dual, shift_factors, storage_bus):
    units = generation.shape[0] // n_bus
    stors = storage_bus.shape[0] // n_bus
    block = flow_dual.shape[0] // n_bus
    hours = charging.shape[0] // 2
    buses = shift_factors.shape[1] // n_bus
    return (
        n_bus % 2 == 0
        and units == stors
        and 4 * units == LANES
        and hours == 16
        and block % LANES == 0
        and buses % LANES == 0
        and shift_factors.shape[0] * buses * 4 <= 2**24
    )


def solution(mesh):
    placed = (
        P("bus", "groups"),
        P("groups", "bus"),
        P("bus", "groups"),
        P("groups", "bus"),
        P(None, "bus"),
        P("bus", "groups"),
        P("bus"),
        P("bus"),
        P("bus"),
        P("bus"),
        P(),
        P(),
        P(),
        P("bus"),
    )
    n_bus = mesh.shape["bus"]

    def whole(*arrays):
        fits = mesh.shape["groups"] == 2 and fits_kernel(
            n_bus, arrays[0], arrays[1], arrays[2], arrays[4], arrays[7]
        )
        return jax.shard_map(
            on_device_kernel if fits else on_device,
            mesh=mesh,
            in_specs=placed,
            out_specs=(P("bus", "groups"), P("groups", "bus"), P("bus", "groups"), P("groups", "bus")),
            check_vma=False,
        )(*arrays)

    return whole
```

time: 338 us -> 58 us (0.17); the launches traced: 334 us -> 57.5 us
  waiting for transfers between devices: 156 us -> 0 us
  matrix products: 92.4 us -> 0 us
  blocking collectives: 64.3 us -> 0 us
  Pallas kernels: 0 us -> 45.5 us
  between operations: 14.4 us -> 0.67 us
  local copies, waits for them, and re-layouts: 2.32 us -> 11.4 us
  other arithmetic: 4.55 us -> 0 us
    reduce_scatter x3 -> x0, waiting for transfers between devices: 156 us -> none  [on_device(): lax.psum_scatter(contract(shift_factors, injected, inner_pair), 'bus', sc...]
    dot_general x18 -> x0, matrix products: 92.4 us -> none  [contract(): lax.dot_general(left, right, dims, precision=highest, preferred_element_t...]
    all_gather x3 -> x0, blocking collectives: 64.3 us -> none  [on_device(): lax.all_gather(flow_dual, 'bus', axis=0, tiled=True)]
    pallas_call x0 -> x1, Pallas kernels: none -> 45.5 us  [on_device_kernel(): pl.pallas_call(functools.partial(iterate_kernel, n_bus), out_shape=(jax.S...]
    unnamed x24 -> x30, local copies, waits for them, and re-layouts: 0.06 us -> 11.4 us
    sub x6 -> x0, other arithmetic: 3.43 us -> none  [clip_dual(): shifted - step_size * jnp.clip(shifted / step_size, low_bound, high_bound)]
  transfers between devices with their start and end apart: 3 -> 0, of which waited for: 3 -> 0; matrix products, arithmetic and copies ran while one was open for 1% -> 0% of each run, Pallas kernels for 0% -> 0%
where the time goes in v1:
time: 58 us; the launch traced here: 57.5 us
  Pallas kernels  45.5 us (78%)
  local copies, waits for them, and re-layouts  11.4 us (20%)
  between operations  0.67 us (1%)
    pallas_call x1, Pallas kernels, on_device_kernel(): pl.pallas_call(functools.partial(iterate_kernel, n_bus), out_shape=(jax.S...  45.5 us
    unnamed x30, local copies, waits for them, and re-layouts  11.4 us

profile of v1, /device:TPU:0, one launch (start us, length us, event | category | flops | bytes accessed | tf_op | source)
XLA Modules:
  0.0 57.5 jit_solution(11805149026910499770)
XLA Ops:
  0.6 0.0 copy-start
  0.6 0.8 %copy-done = s32[1024,16]{0,1:T(8,128)S(1)} copy-done((s32[1024,16]{0,1:T(8,128)S(1)}, s32[1024,16]{0,1:T(8,128)}, u32[]{:S(2)}) %copy-start) | copy-done | bytes 65560
  1.5 0.0 copy-start.1
  1.5 0.7 %copy-done.1 = f32[256,16]{0,1:T(8,128)S(1)} copy-done((f32[256,16]{0,1:T(8,128)S(1)}, f32[256,16]{0,1:T(8,128)}, u32[]{:S(2)}) %copy-start.1) | copy-done | bytes 16408
  2.2 0.0 copy-start.2
  2.2 0.7 %copy-done.2 = f32[32,16]{0,1:T(8,128)S(1)} copy-done((f32[32,16]{0,1:T(8,128)S(1)}, f32[32,16]{0,1:T(8,128)}, u32[]{:S(2)}) %copy-start.2) | copy-done | bytes 2072
  2.9 0.0 copy-start.3
  2.9 0.7 %copy-done.3 = f32[16,32]{1,0:T(8,128)S(1)} copy-done((f32[16,32]{1,0:T(8,128)S(1)}, f32[16,32]{1,0:T(8,128)}, u32[]{:S(2)}) %copy-start.3) | copy-done | bytes 2072
  3.6 0.0 copy-start.4
  3.6 0.7 %copy-done.4 = f32[16,32]{1,0:T(8,128)S(1)} copy-done((f32[16,32]{1,0:T(8,128)S(1)}, f32[16,32]{1,0:T(8,128)}, u32[]{:S(2)}) %copy-start.4) | copy-done | bytes 2072
  4.3 0.0 copy-start.5
  4.3 0.7 %copy-done.5 = f32[512]{0:T(512)S(1)} copy-done((f32[512]{0:T(512)S(1)}, f32[512]{0:T(512)}, u32[]{:S(2)}) %copy-start.5) | copy-done | bytes 2072
  5.0 0.0 copy-start.6
  5.0 0.7 %copy-done.6 = f32[512]{0:T(512)S(1)} copy-done((f32[512]{0:T(512)S(1)}, f32[512]{0:T(512)}, u32[]{:S(2)}) %copy-start.6) | copy-done | bytes 2072
  5.7 0.0 copy-start.7
  5.7 0.7 %copy-done.7 = f32[512]{0:T(512)S(1)} copy-done((f32[512]{0:T(512)S(1)}, f32[512]{0:T(512)}, u32[]{:S(2)}) %copy-start.7) | copy-done | bytes 2072
  6.3 0.0 copy-start.8
  6.3 0.7 %copy-done.8 = f32[256]{0:T(256)S(1)} copy-done((f32[256]{0:T(256)S(1)}, f32[256]{0:T(256)}, u32[]{:S(2)}) %copy-start.8) | copy-done | bytes 1048
  7.0 0.0 copy-start.9
  7.0 0.7 %copy-done.9 = s32[32]{0:T(128)S(1)} copy-done((s32[32]{0:T(128)S(1)}, s32[32]{0:T(128)}, u32[]{:S(2)}) %copy-start.9) | copy-done | bytes 152
  7.7 0.0 copy-start.10
  7.7 0.7 %copy-done.10 = s32[32]{0:T(128)S(1)} copy-done((s32[32]{0:T(128)S(1)}, s32[32]{0:T(128)}, u32[]{:S(2)}) %copy-start.10) | copy-done | bytes 152
  8.3 0.0 copy-start.11
  8.3 0.7 %copy-done.11 = f32[32]{0:T(128)S(1)} copy-done((f32[32]{0:T(128)S(1)}, f32[32]{0:T(128)}, u32[]{:S(2)}) %copy-start.11) | copy-done | bytes 152
  9.0 0.0 copy-start.12
  9.0 0.7 %copy-done.12 = f32[32]{0:T(128)S(1)} copy-done((f32[32]{0:T(128)S(1)}, f32[32]{0:T(128)}, u32[]{:S(2)}) %copy-start.12) | copy-done | bytes 152
  9.6 45.5 %shard_map.165 = (f32[16,32]{1,0:T(8,128)S(1)}, f32[16,32]{1,0:T(8,128)S(1)}, f32[16,256]{1,0:T(8,128)S(1)}, f32[16,32]{1,0:T(8,128)S(1)}) custom-call(f32[16,32]{1,0:T(8,128)S(1)} %bitcast.16, f32[16,32]{1,0:T(8,128)S(1)} %copy-done.3, f32[16,256]{1,0:T(8,128)S(1)} %bitcast.14, f32[16,32]{1,0:T(8,128)S(1)} %copy-done.4, f32[4096,1024]{1,0:T(8,128)} %factors_ref.1, ...), custom_call_target="tpu_custom_call" | custom-call | tf_op jit(solution)/shard_map/pallas_call | solution.py:362
  55.1 0.6 %copy.22 = f32[32,16]{0,1:T(8,128)} copy(f32[32,16]{0,1:T(8,128)S(1)} %bitcast.17) | data formatting | bytes 4096
  55.7 0.6 %copy.23 = f32[16,32]{1,0:T(8,128)} copy(f32[16,32]{1,0:T(8,128)S(1)} %get-tuple-element.17) | data formatting | bytes 4096
  56.3 0.6 %copy.24 = f32[256,16]{0,1:T(8,128)} copy(f32[256,16]{0,1:T(8,128)S(1)} %bitcast.15) | data formatting | bytes 32768
  56.9 0.6 %copy.25 = f32[16,32]{1,0:T(8,128)} copy(f32[16,32]{1,0:T(8,128)S(1)} %get-tuple-element.19) | data formatting | bytes 4096
Async XLA Ops:
  0.6 0.8 %copy-start = (s32[1024,16]{0,1:T(8,128)S(1)}, s32[1024,16]{0,1:T(8,128)}, u32[]{:S(2)}) copy-start(s32[1024,16]{0,1:T(8,128)} %param.19) | copy-start | bytes 196612
  1.5 0.7 %copy-start.1 = (f32[256,16]{0,1:T(8,128)S(1)}, f32[256,16]{0,1:T(8,128)}, u32[]{:S(2)}) copy-start(f32[256,16]{0,1:T(8,128)} %param.16) | copy-start | bytes 49156
  2.2 0.7 %copy-start.2 = (f32[32,16]{0,1:T(8,128)S(1)}, f32[32,16]{0,1:T(8,128)}, u32[]{:S(2)}) copy-start(f32[32,16]{0,1:T(8,128)} %param.14) | copy-start | bytes 6148
  2.9 0.7 %copy-start.3 = (f32[16,32]{1,0:T(8,128)S(1)}, f32[16,32]{1,0:T(8,128)}, u32[]{:S(2)}) copy-start(f32[16,32]{1,0:T(8,128)} %charge_ref.1) | copy-start | bytes 6148
  3.6 0.7 %copy-start.4 = (f32[16,32]{1,0:T(8,128)S(1)}, f32[16,32]{1,0:T(8,128)}, u32[]{:S(2)}) copy-start(f32[16,32]{1,0:T(8,128)} %energy_ref.1) | copy-start | bytes 6148
  4.3 0.7 %copy-start.5 = (f32[512]{0:T(512)S(1)}, f32[512]{0:T(512)}, u32[]{:S(2)}) copy-start(f32[512]{0:T(512)} %param.24) | copy-start | bytes 6148
  5.0 0.7 %copy-start.6 = (f32[512]{0:T(512)S(1)}, f32[512]{0:T(512)}, u32[]{:S(2)}) copy-start(f32[512]{0:T(512)} %param.25) | copy-start | bytes 6148
  5.7 0.7 %copy-start.7 = (f32[512]{0:T(512)S(1)}, f32[512]{0:T(512)}, u32[]{:S(2)}) copy-start(f32[512]{0:T(512)} %param.26) | copy-start | bytes 6148
  6.3 0.7 %copy-start.8 = (f32[256]{0:T(256)S(1)}, f32[256]{0:T(256)}, u32[]{:S(2)}) copy-start(f32[256]{0:T(256)} %param.27) | copy-start | bytes 3076
  7.0 0.7 %copy-start.9 = (s32[32]{0:T(128)S(1)}, s32[32]{0:T(128)}, u32[]{:S(2)}) copy-start(s32[32]{0:T(128)} %param.20) | copy-start | bytes 388
  7.7 0.7 %copy-start.10 = (s32[32]{0:T(128)S(1)}, s32[32]{0:T(128)}, u32[]{:S(2)}) copy-start(s32[32]{0:T(128)} %param.21) | copy-start | bytes 388
  8.3 0.7 %copy-start.11 = (f32[32]{0:T(128)S(1)}, f32[32]{0:T(128)}, u32[]{:S(2)}) copy-start(f32[32]{0:T(128)} %param.22) | copy-start | bytes 388
  9.0 0.7 %copy-start.12 = (f32[32]{0:T(128)S(1)}, f32[32]{0:T(128)}, u32[]{:S(2)}) copy-start(f32[32]{0:T(128)} %param.23) | copy-start | bytes 388

commit v2 on v1

--- a/solution.py
+++ b/solution.py
@@ -9,6 +9,7 @@
 
 ITERS = 3
 LANES = 128
+VMEM_BYTES = 65472 * 1024
 MESH = pl.DeviceIdType.MESH
 
 primal_step = 0.5
@@ -56,11 +57,27 @@
 
 def iterate_kernel(
     n_bus,
+    gen_hbm,
+    charge_hbm,
+    dual_hbm,
+    energy_hbm,
+    factors_hbm,
+    load_hbm,
+    gen_bus_hbm,
+    stor_bus_hbm,
+    cost_hbm,
+    gen_max_hbm,
+    charge_max_hbm,
+    init_hbm,
+    energy_max_hbm,
+    line_max_hbm,
+    gen_hbm_out,
+    charge_hbm_out,
+    dual_hbm_out,
+    energy_hbm_out,
     gen_ref,
     charge_ref,
-    dual_ref,
     energy_ref,
-    factors_ref,
     load_ref,
     gen_bus_ref,
     stor_bus_ref,
@@ -81,12 +98,15 @@
     cols_send,
     cols_recv,
     weight_buf,
+    turned_buf,
     demand_buf,
     dual_buf,
     flow_send,
     flow_recv,
     price_send,
     price_recv,
+    input_sem,
+    output_sem,
     factors_sem,
     pack_sem,
     cols_sems,
@@ -98,23 +118,59 @@
 ):
     chips = n_bus // 2
     hours, units = gen_ref.shape
-    block = dual_ref.shape[1]
-    buses = factors_ref.shape[1]
+    block = dual_hbm.shape[1]
+    buses = factors_hbm.shape[1]
     half = 2 * units
     width = 2 * half
     me = lax.axis_index("bus")
     core = lax.rem(me, 2)
     chip = lax.div(me, 2)
     sibling = me + 1 - 2 * core
+    far_first = sorted(range(1, chips), key=lambda k: abs(2 * k - chips))
 
     def peer(k):
         return lax.rem(chip + k, chips)
+
+    dual_in = pltpu.make_async_copy(dual_hbm, dual_buf.at[0, chip], input_sem.at[0])
+    fetches = [
+        pltpu.make_async_copy(source, target, input_sem.at[1 + at])
+        for at, (source, target) in enumerate(
+            (
+                (load_hbm, load_ref),
+                (gen_bus_hbm, gen_bus_ref),
+                (stor_bus_hbm, stor_bus_ref),
+                (gen_hbm, gen_ref),
+                (charge_hbm, charge_ref),
+                (energy_hbm, energy_ref),
+                (cost_hbm, cost_ref),
+                (gen_max_hbm, gen_max_ref),
+                (charge_max_hbm, charge_max_ref),
+                (init_hbm, init_ref),
+                (energy_max_hbm, energy_max_ref),
+                (line_max_hbm, line_max_ref),
+            )
+        )
+    ]
+    stores = [
+        pltpu.make_async_copy(source, target, output_sem.at[at])
+        for at, (source, target) in enumerate(
+            (
+                (gen_out, gen_hbm_out),
+                (charge_out, charge_hbm_out),
+                (energy_out, energy_hbm_out),
+                (dual_out, dual_hbm_out),
+            )
+        )
+    ]
+    dual_in.start()
+    for fetch in fetches:
+        fetch.start()
 
     def load_factors(i, parity):
         b = 2 * i + parity
         start = pl.multiple_of(b * block, block)
         return pltpu.make_async_copy(
-            factors_ref.at[pl.ds(start, block), :], factors_buf.at[b], factors_sem.at[b]
+            factors_hbm.at[pl.ds(start, block), :], factors_buf.at[b], factors_sem.at[b]
         )
 
     @pl.loop(0, chips)
@@ -131,12 +187,10 @@
             barrier, inc=1, device_id={"bus": 2 * peer(k) + core}, device_id_type=MESH
         )
     pl.semaphore_signal(barrier, inc=1, device_id={"bus": sibling}, device_id_type=MESH)
-    pl.semaphore_wait(barrier, chips)
 
     def send_dual(t, k):
-        source = dual_ref if t == 0 else dual_buf.at[t, chip]
         return pltpu.make_async_remote_copy(
-            src_ref=source,
+            src_ref=dual_buf.at[t, chip],
             dst_ref=dual_buf.at[t, chip],
             send_sem=dual_send_sem.at[t, k],
             recv_sem=dual_recv_sem.at[t, chip],
@@ -184,26 +238,8 @@
             device_id_type=MESH,
         )
 
-    for k in range(1, chips):
-        send_dual(0, k).start()
-
-    gens = slice(0, units)
-    stors = slice(units, half)
-    pack_own[...] = jnp.zeros_like(pack_own)
-    pack_own[0, :, gens] = gen_ref[...]
-    pack_own[0, :, stors] = charge_ref[...]
-    pack_own[1, :, stors] = energy_ref[...]
-    pack_own[2, 0:1, gens] = cost_ref[...]
-    pack_own[2, 1:2, gens] = gen_max_ref[...]
-    first = me * units
-    lane_start = pl.multiple_of(lax.div(first, LANES) * LANES, LANES)
-    shift = lax.rem(units - lax.rem(first, LANES) + LANES, LANES)
-    for row, ref in ((1, charge_max_ref), (2, init_ref), (3, energy_max_ref)):
-        chunk = jnp.broadcast_to(ref[0:1, pl.ds(lane_start, LANES)], (8, LANES))
-        pack_own[2, row : row + 1, stors] = pltpu.roll(chunk, shift, 1)[0:1, stors]
-    send_pack = to_sibling(pack_own, pack_sib, pack_sem)
-    send_pack.start()
-
+    for fetch in fetches[:3]:
+        fetch.wait()
     pack_index = jnp.full((8, LANES), -1, jnp.int32)
     lane8 = lax.broadcasted_iota(jnp.int32, (8, LANES), 1)
     for at, ref in ((0, gen_bus_ref), (units, stor_bus_ref)):
@@ -220,15 +256,40 @@
         ],
         axis=0,
     )
-    place_buf[...] = (onehot + loads.T).astype(jnp.bfloat16)
-
-    def take_columns(b):
+    place = onehot + loads.T
+    place_buf[0] = place.astype(jnp.bfloat16)
+    place_buf[1] = pltpu.roll(place, half, 1).astype(jnp.bfloat16)
+
+    for fetch in fetches[3:]:
+        fetch.wait()
+    gens = slice(0, units)
+    stors = slice(units, half)
+    pack_own[...] = jnp.zeros_like(pack_own)
+    pack_own[0, :, gens] = gen_ref[...]
+    pack_own[0, :, stors] = charge_ref[...]
+    pack_own[1, :, stors] = energy_ref[...]
+    pack_own[2, 0:1, gens] = cost_ref[...]
+    pack_own[2, 1:2, gens] = gen_max_ref[...]
+    first = me * units
+    lane_start = pl.multiple_of(lax.div(first, LANES) * LANES, LANES)
+    shift = lax.rem(units - lax.rem(first, LANES) + LANES, LANES)
+    for row, ref in ((1, charge_max_ref), (2, init_ref), (3, energy_max_ref)):
+        chunk = jnp.broadcast_to(ref[0:1, pl.ds(lane_start, LANES)], (8, LANES))
+        pack_own[2, row : row + 1, stors] = pltpu.roll(chunk, shift, 1)[0:1, stors]
+
+    pl.semaphore_wait(barrier, chips)
+    dual_in.wait()
+    for k in far_first:
+        send_dual(0, k).start()
+    send_pack = to_sibling(pack_own, pack_sib, pack_sem)
+    send_pack.start()
+
+    def take_columns(b, placed):
         high, low = split_bf16(factors_buf[b])
-        place = place_buf[...]
-        taken = jnp.dot(high, place, preferred_element_type=jnp.float32) + jnp.dot(
+        place = place_buf[placed]
+        return jnp.dot(high, place, preferred_element_type=jnp.float32) + jnp.dot(
             low, place, preferred_element_type=jnp.float32
         )
-        return taken.T[: half + hours]
 
     def swap_columns(i):
         return pltpu.make_async_remote_copy(
@@ -240,22 +301,46 @@
             device_id_type=MESH,
         )
 
-    @pl.loop(0, chips)
-    def _(i):
-        load_factors(i, 1 - core).wait()
-        cols_send[i] = take_columns(2 * i + 1 - core)
-        swap_columns(i).start()
-
-    @pl.loop(0, chips)
-    def _(i):
-        load_factors(i, core).wait()
-        mine = take_columns(2 * i + core)
-        swap_columns(i).wait()
-        other = cols_recv[i]
-        high, low = split_bf16(jnp.concatenate([mine[:half], other[:half]], axis=0))
-        weight_buf[i, 0:width] = high
-        weight_buf[i, width : 2 * width] = low
-        demand_buf[i] = load_unit * (mine[half:] + other[half:])
+    together = 2 if chips % 2 == 0 else 1
+
+    @pl.loop(0, chips // together)
+    def _(step):
+        turns = [step * together + j for j in range(together)]
+        for i in turns:
+            load_factors(i, 1 - core).wait()
+        for i in turns:
+            cols_send[i] = take_columns(2 * i + 1 - core, 1)
+        for i in turns:
+            swap_columns(i).start()
+
+    for k in reversed(far_first):
+        recv_dual(0, peer(chips - k)).wait_recv()
+
+    def collect(step, total):
+        turns = [step * together + j for j in range(together)]
+        for i in turns:
+            load_factors(i, core).wait()
+        for i in turns:
+            swap_columns(i).wait()
+        for i in turns:
+            mine = take_columns(2 * i + core, 0)
+            other = cols_recv[i]
+            lane_at = lax.broadcasted_iota(jnp.int32, mine.shape, 1)
+            columns = jnp.where(lane_at < half, mine, other)
+            turned = jnp.concatenate(split_bf16(columns), axis=1)
+            turned_buf[i] = turned
+            high, low = split_bf16(columns.T)
+            weight_buf[i, 0:width] = high
+            weight_buf[i, width : 2 * width] = low
+            demand = mine + pltpu.roll(other, half, 1)
+            demand_buf[i] = load_unit * demand.T[half : half + hours]
+            pieces = jnp.concatenate(split_bf16(dual_buf[0, i]), axis=0)
+            total = total + jnp.dot(pieces, turned, preferred_element_type=jnp.float32)
+        return total
+
+    total = lax.fori_loop(
+        0, chips // together, collect, jnp.zeros((2 * hours, 2 * width), jnp.float32)
+    )
 
     send_pack.wait()
     state = pack_own[0] + pltpu.roll(pack_sib[0], half, 1)
@@ -266,22 +351,21 @@
     is_gen = lax.rem(lane, half) < units
     lower = jnp.where(is_gen, 0.0, -upper)
     later = running_sum(energy_dual, True)
-    own_dual = dual_ref[...]
+    own_dual = dual_buf[0, chip]
     line_max = line_max_ref[...]
 
     for t in range(ITERS):
-        total = jnp.zeros((2 * hours, 2 * width), jnp.float32)
-        for k in range(chips):
-            c = peer(chips - k)
-            if k == 0:
-                dual = own_dual
-            else:
-                recv_dual(t, c).wait_recv()
-                dual = dual_buf[t, c]
-            pieces = jnp.concatenate(split_bf16(dual), axis=0)
-            total = total + lax.dot_general(
-                pieces, weight_buf[c], across_second, preferred_element_type=jnp.float32
-            )
+        if t > 0:
+            total = jnp.zeros((2 * hours, 2 * width), jnp.float32)
+            for k in [0] + far_first[::-1]:
+                c = peer(chips - k)
+                if k == 0:
+                    dual = own_dual
+                else:
+                    recv_dual(t, c).wait_recv()
+                    dual = dual_buf[t, c]
+                pieces = jnp.concatenate(split_bf16(dual), axis=0)
+                total = total + jnp.dot(pieces, turned_buf[c], preferred_element_type=jnp.float32)
         total = total[:hours] + total[hours:]
         part = total[:, :width] + total[:, width:]
         price_send[t] = part
@@ -303,32 +387,52 @@
             out = jnp.dot(pieces, weight_buf[c], preferred_element_type=jnp.float32)
             return out[:hours] + out[hours:] - demand_buf[c]
 
-        for k in range(1, chips):
+        for k in far_first:
             flow_send[t, k] = flows(peer(k))
             send_flow(t, k).start()
         line_flows = flows(chip)
+        if t + 1 == ITERS:
+            gen_out[...] = state[:, gens]
+            charge_out[...] = state[:, stors]
+            stores[0].start()
+            stores[1].start()
         energy = start_energy + efficiency * interval * running_sum(bar, False)
         energy_dual = clip_dual(energy_dual + energy_step * energy, energy_step, 0.0, energy_limit)
         if t + 1 < ITERS:
             later = running_sum(energy_dual, True)
-        for k in range(1, chips):
+        else:
+            energy_out[...] = energy_dual[:, stors]
+            stores[2].start()
+        for k in far_first[::-1]:
             c = peer(chips - k)
             recv_flow(t, c).wait_recv()
             line_flows = line_flows + flow_recv[t, c]
         own_dual = clip_dual(own_dual + dual_step * line_flows, dual_step, -line_max, line_max)
         if t + 1 < ITERS:
             dual_buf[t + 1, chip] = own_dual
-            for k in range(1, chips):
+            for k in far_first:
                 send_dual(t + 1, k).start()
 
     dual_out[...] = own_dual
-    gen_out[...] = state[:, gens]
-    charge_out[...] = state[:, stors]
-    energy_out[...] = energy_dual[:, stors]
+    stores[3].start()
     for t in range(ITERS):
         for k in range(1, chips):
             send_dual(t, k).wait_send()
             send_flow(t, k).wait_send()
+    for store in stores:
+        store.wait()
+
+
+def store_kernel(*refs):
+    count = len(refs) // 2
+    sems = refs[-1]
+    copies = [
+        pltpu.make_async_copy(refs[at], refs[count + at], sems.at[at]) for at in range(count)
+    ]
+    for copy in copies:
+        copy.start()
+    for copy in copies:
+        copy.wait()
 
 
 def on_device_kernel(
@@ -354,48 +458,10 @@
     chips = n_bus // 2
     half = 2 * units
     width = 2 * half
-    vmem = pl.BlockSpec(memory_space=pltpu.VMEM)
-    in_specs = [vmem] * 14
-    in_specs[4] = pl.BlockSpec(memory_space=pltpu.HBM)
+    hbm = pl.BlockSpec(memory_space=pltpu.HBM)
     f32 = jnp.float32
     dma = pltpu.SemaphoreType.DMA
-    gen_new, charge_new, dual_new, energy_new = pl.pallas_call(
-        functools.partial(iterate_kernel, n_bus),
-        out_shape=(
-            jax.ShapeDtypeStruct((hours, units), f32),
-            jax.ShapeDtypeStruct((hours, units), f32),
-            jax.ShapeDtypeStruct((hours, block), f32),
-            jax.ShapeDtypeStruct((hours, units), f32),
-        ),
-        in_specs=in_specs,
-        out_specs=(vmem,) * 4,
-        scratch_shapes=[
-            pltpu.VMEM((n_bus, block, buses), f32),
-            pltpu.VMEM((buses, LANES), jnp.bfloat16),
-            pltpu.VMEM((3, hours, width), f32),
-            pltpu.VMEM((3, hours, width), f32),
-            pltpu.VMEM((chips, half + hours, block), f32),
-            pltpu.VMEM((chips, half + hours, block), f32),
-            pltpu.VMEM((chips, 2 * width, block), jnp.bfloat16),
-            pltpu.VMEM((chips, hours, block), f32),
-            pltpu.VMEM((ITERS, chips, hours, block), f32),
-            pltpu.VMEM((ITERS, chips, hours, block), f32),
-            pltpu.VMEM((ITERS, chips, hours, block), f32),
-            pltpu.VMEM((ITERS, hours, width), f32),
-            pltpu.VMEM((ITERS, hours, width), f32),
-            dma((n_bus,)),
-            dma((2,)),
-            dma((2, chips)),
-            dma((ITERS, chips)),
-            dma((ITERS, chips)),
-            dma((ITERS, chips)),
-            dma((ITERS, chips)),
-            dma((ITERS, 2)),
-        ],
-        compiler_params=pltpu.CompilerParams(
-            collective_id=0, has_side_effects=True, vmem_limit_bytes=52 * 1024 * 1024
-        ),
-    )(
+    arrays = (
         generation.T,
         charging,
         flow_dual.T,
@@ -411,6 +477,61 @@
         energy_max[None, :],
         line_max[None, :],
     )
+    out_shape = (
+        jax.ShapeDtypeStruct((hours, units), f32),
+        jax.ShapeDtypeStruct((hours, units), f32),
+        jax.ShapeDtypeStruct((hours, block), f32),
+        jax.ShapeDtypeStruct((hours, units), f32),
+    )
+    results = pl.pallas_call(
+        functools.partial(iterate_kernel, n_bus),
+        out_shape=out_shape,
+        in_specs=[hbm] * len(arrays),
+        out_specs=(hbm,) * 4,
+        scratch_shapes=[
+            pltpu.VMEM(array.shape, array.dtype)
+            for at, array in enumerate(arrays)
+            if at not in (2, 4)
+        ]
+        + [pltpu.VMEM(result.shape, f32) for result in out_shape]
+        + [
+            pltpu.VMEM((n_bus, block, buses), f32),
+            pltpu.VMEM((2, buses, LANES), jnp.bfloat16),
+            pltpu.VMEM((3, hours, width), f32),
+            pltpu.VMEM((3, hours, width), f32),
+            pltpu.VMEM((chips, block, LANES), f32),
+            pltpu.VMEM((chips, block, LANES), f32),
+            pltpu.VMEM((chips, 2 * width, block), jnp.bfloat16),
+            pltpu.VMEM((chips, block, 2 * width), jnp.bfloat16),
+            pltpu.VMEM((chips, hours, block), f32),
+            pltpu.VMEM((ITERS, chips, hours, block), f32),
+            pltpu.VMEM((ITERS, chips, hours, block), f32),
+            pltpu.VMEM((ITERS, chips, hours, block), f32),
+            pltpu.VMEM((ITERS, hours, width), f32),
+            pltpu.VMEM((ITERS, hours, width), f32),
+            dma((len(arrays) - 1,)),
+            dma((4,)),
+            dma((n_bus,)),
+            dma((2,)),
+            dma((2, chips)),
+            dma((ITERS, chips)),
+            dma((ITERS, chips)),
+            dma((ITERS, chips)),
+            dma((ITERS, chips)),
+            dma((ITERS, 2)),
+        ],
+        compiler_params=pltpu.CompilerParams(
+            collective_id=0, has_side_effects=True, vmem_limit_bytes=VMEM_BYTES
+        ),
+    )(*arrays)
+    gen_new, charge_new, dual_new, energy_new = pl.pallas_call(
+        store_kernel,
+        out_shape=out_shape,
+        in_specs=[hbm] * 4,
+        out_specs=(hbm,) * 4,
+        scratch_shapes=[dma((4,))],
+        compiler_params=pltpu.CompilerParams(vmem_limit_bytes=VMEM_BYTES),
+    )(*results)
     return gen_new.T, charge_new, dual_new.T, energy_new
 
 

time: 58 us -> 51.3 us (0.88)
  local copies, waits for them, and re-layouts: 11.4 us -> 0 us
  Pallas kernels: 45.5 us -> 50.5 us
    unnamed x30 -> x0, local copies, waits for them, and re-layouts: 11.4 us -> none
    pallas_call x1 -> x2, Pallas kernels: 45.5 us -> 50.5 us  [the longest x1 48.1 us: on_device_kernel(): pl.pallas_call(functools.partial(iterate_kernel, n_bus), out_shape=out_sh...]
where the time goes in v2:
time: 51.3 us; the launch traced here: 51.2 us
  Pallas kernels  50.5 us (98%)
  between operations  0.64 us (1%)
    pallas_call x1, Pallas kernels, on_device_kernel(): pl.pallas_call(functools.partial(iterate_kernel, n_bus), out_shape=out_sh...  48.1 us
    pallas_call x1, Pallas kernels, on_device_kernel(): pl.pallas_call(store_kernel, out_shape=out_shape, in_specs=[hbm] * 4, out...  2.38 us

profile of v2, /device:TPU:0, one launch (start us, length us, event | category | flops | bytes accessed | tf_op | source)
XLA Modules:
  0.0 51.2 jit_solution(1278127702629588730)
XLA Ops:
  0.6 48.1 %shard_map.165 = (f32[16,32]{1,0:T(8,128)}, f32[16,32]{1,0:T(8,128)}, f32[16,256]{1,0:T(8,128)}, f32[16,32]{1,0:T(8,128)}) custom-call(f32[16,32]{1,0:T(8,128)} %bitcast.15, f32[16,32]{1,0:T(8,128)} %charge_hbm.1, f32[16,256]{1,0:T(8,128)} %bitcast.14, f32[16,32]{1,0:T(8,128)} %energy_hbm.1, f32[4096,1024]{1,0:T(8,128)} %factors_hbm.1, s32[16,1024]{1,0:T(8,128)} %bitcast.13, ...), custom_call_target="tpu_custom_call" | custom-call | tf_op jit(solution)/shard_map/pallas_call | solution.py:486
  48.8 2.4 %shard_map.166 = (f32[16,32]{1,0:T(8,128)}, f32[16,32]{1,0:T(8,128)}, f32[16,256]{1,0:T(8,128)}, f32[16,32]{1,0:T(8,128)}) custom-call(f32[16,32]{1,0:T(8,128)} %get-tuple-element.12.refs_0_, f32[16,32]{1,0:T(8,128)} %get-tuple-element.13.refs_1_, f32[16,256]{1,0:T(8,128)} %get-tuple-element.14.refs_2_, f32[16,32]{1,0:T(8,128)} %get-tuple-element.15.refs_3_), custom_call_target="tpu_custom_call" | custom-call | tf_op jit(solution)/shard_map/pallas_call | solution.py:527

commit v3 on v2

--- a/solution.py
+++ b/solution.py
@@ -9,6 +9,7 @@
 
 ITERS = 3
 LANES = 128
+PARTS = 2
 VMEM_BYTES = 65472 * 1024
 MESH = pl.DeviceIdType.MESH
 
@@ -188,42 +189,47 @@
         )
     pl.semaphore_signal(barrier, inc=1, device_id={"bus": sibling}, device_id_type=MESH)
 
-    def send_dual(t, k):
+    part_rows = hours // PARTS
+
+    def rows(part):
+        return slice(part * part_rows, (part + 1) * part_rows)
+
+    def send_dual(t, k, part):
         return pltpu.make_async_remote_copy(
-            src_ref=dual_buf.at[t, chip],
-            dst_ref=dual_buf.at[t, chip],
-            send_sem=dual_send_sem.at[t, k],
-            recv_sem=dual_recv_sem.at[t, chip],
+            src_ref=dual_buf.at[t, chip, rows(part)],
+            dst_ref=dual_buf.at[t, chip, rows(part)],
+            send_sem=dual_send_sem.at[t, part, k],
+            recv_sem=dual_recv_sem.at[t, part, chip],
             device_id={"bus": 2 * peer(k) + core},
             device_id_type=MESH,
         )
 
-    def recv_dual(t, c):
+    def recv_dual(t, c, part):
         return pltpu.make_async_remote_copy(
-            src_ref=dual_buf.at[t, c],
-            dst_ref=dual_buf.at[t, c],
-            send_sem=dual_send_sem.at[t, 0],
-            recv_sem=dual_recv_sem.at[t, c],
+            src_ref=dual_buf.at[t, c, rows(part)],
+            dst_ref=dual_buf.at[t, c, rows(part)],
+            send_sem=dual_send_sem.at[t, part, 0],
+            recv_sem=dual_recv_sem.at[t, part, c],
             device_id={"bus": sibling},
             device_id_type=MESH,
         )
 
-    def send_flow(t, k):
+    def send_flow(t, k, part):
         return pltpu.make_async_remote_copy(
-            src_ref=flow_send.at[t, k],
-            dst_ref=flow_recv.at[t, chip],
-            send_sem=flow_send_sem.at[t, k],
-            recv_sem=flow_recv_sem.at[t, chip],
+            src_ref=flow_send.at[t, k, rows(part)],
+            dst_ref=flow_recv.at[t, chip, rows(part)],
+            send_sem=flow_send_sem.at[t, part, k],
+            recv_sem=flow_recv_sem.at[t, part, chip],
             device_id={"bus": 2 * peer(k) + core},
             device_id_type=MESH,
         )
 
-    def recv_flow(t, c):
+    def recv_flow(t, c, part):
         return pltpu.make_async_remote_copy(
-            src_ref=flow_recv.at[t, c],
-            dst_ref=flow_recv.at[t, c],
-            send_sem=flow_send_sem.at[t, 0],
-            recv_sem=flow_recv_sem.at[t, c],
+            src_ref=flow_recv.at[t, c, rows(part)],
+            dst_ref=flow_recv.at[t, c, rows(part)],
+            send_sem=flow_send_sem.at[t, part, 0],
+            recv_sem=flow_recv_sem.at[t, part, c],
             device_id={"bus": sibling},
             device_id_type=MESH,
         )
@@ -280,7 +286,8 @@
     pl.semaphore_wait(barrier, chips)
     dual_in.wait()
     for k in far_first:
-        send_dual(0, k).start()
+        for part in range(PARTS):
+            send_dual(0, k, part).start()
     send_pack = to_sibling(pack_own, pack_sib, pack_sem)
     send_pack.start()
 
@@ -314,7 +321,8 @@
             swap_columns(i).start()
 
     for k in reversed(far_first):
-        recv_dual(0, peer(chips - k)).wait_recv()
+        for part in range(PARTS):
+            recv_dual(0, peer(chips - k), part).wait_recv()
 
     def collect(step, total):
         turns = [step * together + j for j in range(together)]
@@ -351,88 +359,124 @@
     is_gen = lax.rem(lane, half) < units
     lower = jnp.where(is_gen, 0.0, -upper)
     later = running_sum(energy_dual, True)
-    own_dual = dual_buf[0, chip]
+    own_dual = [dual_buf[0, chip, rows(part)] for part in range(PARTS)]
+    state = [state[rows(part)] for part in range(PARTS)]
+    is_gen_part, lower_part = is_gen[:part_rows], lower[:part_rows]
     line_max = line_max_ref[...]
 
+    def stacked(values):
+        high = values.astype(jnp.bfloat16).astype(jnp.float32)
+        return jnp.concatenate([high, values - high], axis=0).astype(jnp.bfloat16)
+
+    def swap_prices(t, part):
+        return to_sibling(
+            price_send.at[t, rows(part)], price_recv.at[t, rows(part)], price_sem.at[t, part]
+        )
+
     for t in range(ITERS):
-        if t > 0:
-            total = jnp.zeros((2 * hours, 2 * width), jnp.float32)
-            for k in [0] + far_first[::-1]:
-                c = peer(chips - k)
-                if k == 0:
-                    dual = own_dual
-                else:
-                    recv_dual(t, c).wait_recv()
-                    dual = dual_buf[t, c]
-                pieces = jnp.concatenate(split_bf16(dual), axis=0)
-                total = total + jnp.dot(pieces, turned_buf[c], preferred_element_type=jnp.float32)
-        total = total[:hours] + total[hours:]
-        part = total[:, :width] + total[:, width:]
-        price_send[t] = part
-        swap_prices = to_sibling(price_send.at[t], price_recv.at[t], price_sem.at[t])
-        swap_prices.start()
-        swap_prices.wait()
-        prices = part + pltpu.roll(price_recv[t], half, 1)
-
-        gradient = jnp.where(is_gen, cost + prices, efficiency * interval * later - prices)
-        step = jnp.clip(state - primal_step * gradient, lower, upper)
-        bar = 2.0 * step - state
-        state = step
-        high, low = split_bf16(jnp.where(is_gen, bar, -bar))
-        pieces = jnp.concatenate(
-            [jnp.concatenate([high, high], axis=1), jnp.concatenate([low, low], axis=1)], axis=0
-        )
-
-        def flows(c):
-            out = jnp.dot(pieces, weight_buf[c], preferred_element_type=jnp.float32)
-            return out[:hours] + out[hours:] - demand_buf[c]
-
-        for k in far_first:
-            flow_send[t, k] = flows(peer(k))
-            send_flow(t, k).start()
-        line_flows = flows(chip)
+        partial = [None] * PARTS
+        for part in range(PARTS):
+            if t == 0:
+                both = total[:hours] + total[hours:]
+                both = both[rows(part)]
+            else:
+                total = jnp.zeros((2 * part_rows, 2 * width), jnp.float32)
+                for k in [0] + far_first[::-1]:
+                    c = peer(chips - k)
+                    if k == 0:
+                        dual = own_dual[part]
+                    else:
+                        recv_dual(t, c, part).wait_recv()
+                        dual = dual_buf[t, c, rows(part)]
+                    total = total + jnp.dot(
+                        stacked(dual), turned_buf[c], preferred_element_type=jnp.float32
+                    )
+                both = total[:part_rows] + total[part_rows:]
+            partial[part] = both[:, :width] + both[:, width:]
+            price_send[t, rows(part)] = partial[part]
+            swap_prices(t, part).start()
+
+        bars = []
+        line_flows = []
+        for part in range(PARTS):
+            swap_prices(t, part).wait()
+            prices = partial[part] + pltpu.roll(price_recv[t, rows(part)], half, 1)
+            pull = efficiency * interval * later[rows(part)]
+            gradient = jnp.where(is_gen_part, cost + prices, pull - prices)
+            step = jnp.clip(state[part] - primal_step * gradient, lower_part, upper)
+            bar = 2.0 * step - state[part]
+            state[part] = step
+            bars.append(bar)
+            pieces = stacked(jnp.where(is_gen_part, bar, -bar))
+            pieces = jnp.concatenate([pieces, pieces], axis=1)
+
+            def flows(c):
+                out = jnp.dot(pieces, weight_buf[c], preferred_element_type=jnp.float32)
+                return out[:part_rows] + out[part_rows:] - demand_buf[c, rows(part)]
+
+            for k in far_first:
+                flow_send[t, k, rows(part)] = flows(peer(k))
+                send_flow(t, k, part).start()
+            line_flows.append(flows(chip))
+
         if t + 1 == ITERS:
-            gen_out[...] = state[:, gens]
-            charge_out[...] = state[:, stors]
+            for part in range(PARTS):
+                gen_out[rows(part)] = state[part][:, gens]
+                charge_out[rows(part)] = state[part][:, stors]
             stores[0].start()
             stores[1].start()
-        energy = start_energy + efficiency * interval * running_sum(bar, False)
+        so_far = running_sum(jnp.concatenate(bars, axis=0), False)
+        energy = start_energy + efficiency * interval * so_far
         energy_dual = clip_dual(energy_dual + energy_step * energy, energy_step, 0.0, energy_limit)
         if t + 1 < ITERS:
             later = running_sum(energy_dual, True)
         else:
             energy_out[...] = energy_dual[:, stors]
             stores[2].start()
-        for k in far_first[::-1]:
-            c = peer(chips - k)
-            recv_flow(t, c).wait_recv()
-            line_flows = line_flows + flow_recv[t, c]
-        own_dual = clip_dual(own_dual + dual_step * line_flows, dual_step, -line_max, line_max)
-        if t + 1 < ITERS:
-            dual_buf[t + 1, chip] = own_dual
-            for k in far_first:
-                send_dual(t + 1, k).start()
-
-    dual_out[...] = own_dual
+
+        for part in range(PARTS):
+            flow = line_flows[part]
+            for k in far_first[::-1]:
+                c = peer(chips - k)
+                recv_flow(t, c, part).wait_recv()
+                flow = flow + flow_recv[t, c, rows(part)]
+            own_dual[part] = clip_dual(
+                own_dual[part] + dual_step * flow, dual_step, -line_max, line_max
+            )
+            if t + 1 < ITERS:
+                dual_buf[t + 1, chip, rows(part)] = own_dual[part]
+                for k in far_first:
+                    send_dual(t + 1, k, part).start()
+            else:
+                dual_out[rows(part)] = own_dual[part]
+
     stores[3].start()
     for t in range(ITERS):
-        for k in range(1, chips):
-            send_dual(t, k).wait_send()
-            send_flow(t, k).wait_send()
+        for part in range(PARTS):
+            for k in range(1, chips):
+                send_dual(t, k, part).wait_send()
+                send_flow(t, k, part).wait_send()
     for store in stores:
         store.wait()
 
 
 def store_kernel(*refs):
-    count = len(refs) // 2
+    count = len(refs) // 3
     sems = refs[-1]
-    copies = [
-        pltpu.make_async_copy(refs[at], refs[count + at], sems.at[at]) for at in range(count)
+    fetches = [
+        pltpu.make_async_copy(refs[at], refs[2 * count + at], sems.at[0, at]) for at in range(count)
     ]
-    for copy in copies:
-        copy.start()
-    for copy in copies:
-        copy.wait()
+    stores = [
+        pltpu.make_async_copy(refs[2 * count + at], refs[count + at], sems.at[1, at])
+        for at in range(count)
+    ]
+    for fetch in fetches:
+        fetch.start()
+    for fetch, store in zip(fetches, stores):
+        fetch.wait()
+        store.start()
+    for store in stores:
+        store.wait()
 
 
 def on_device_kernel(
@@ -514,11 +558,11 @@
             dma((n_bus,)),
             dma((2,)),
             dma((2, chips)),
-            dma((ITERS, chips)),
-            dma((ITERS, chips)),
-            dma((ITERS, chips)),
-            dma((ITERS, chips)),
-            dma((ITERS, 2)),
+            dma((ITERS, PARTS, chips)),
+            dma((ITERS, PARTS, chips)),
+            dma((ITERS, PARTS, chips)),
+            dma((ITERS, PARTS, chips)),
+            dma((ITERS, PARTS, 2)),
         ],
         compiler_params=pltpu.CompilerParams(
             collective_id=0, has_side_effects=True, vmem_limit_bytes=VMEM_BYTES
@@ -529,7 +573,7 @@
         out_shape=out_shape,
         in_specs=[hbm] * 4,
         out_specs=(hbm,) * 4,
-        scratch_shapes=[dma((4,))],
+        scratch_shapes=[pltpu.VMEM(result.shape, f32) for result in out_shape] + [dma((2, 4))],
         compiler_params=pltpu.CompilerParams(vmem_limit_bytes=VMEM_BYTES),
     )(*results)
     return gen_new.T, charge_new, dual_new.T, energy_new

time: 51.3 us -> 49.6 us (0.967)
  Pallas kernels: 50.5 us -> 48.8 us
    pallas_call x1, Pallas kernels: 2.38 us -> 1.43 us  [on_device_kernel(): pl.pallas_call(store_kernel, out_shape=out_shape, in_specs=[hbm] * 4, out...]
    pallas_call x1, Pallas kernels: 48.1 us -> 47.3 us  [on_device_kernel(): pl.pallas_call(functools.partial(iterate_kernel, n_bus), out_shape=out_sh...]
where the time goes in v3:
time: 49.6 us; the launch traced here: 49.4 us
  Pallas kernels  48.8 us (98%)
  between operations  0.64 us (1%)
    pallas_call x1, Pallas kernels, on_device_kernel(): pl.pallas_call(functools.partial(iterate_kernel, n_bus), out_shape=out_sh...  47.3 us
    pallas_call x1, Pallas kernels, on_device_kernel(): pl.pallas_call(store_kernel, out_shape=out_shape, in_specs=[hbm] * 4, out...  1.43 us

profile of v3, /device:TPU:0, one launch (start us, length us, event | category | flops | bytes accessed | tf_op | source)
XLA Modules:
  0.0 49.4 jit_solution(4734440429264776813)
XLA Ops:
  0.6 47.3 %shard_map.165 = (f32[16,32]{1,0:T(8,128)}, f32[16,32]{1,0:T(8,128)}, f32[16,256]{1,0:T(8,128)}, f32[16,32]{1,0:T(8,128)}) custom-call(f32[16,32]{1,0:T(8,128)} %bitcast.15, f32[16,32]{1,0:T(8,128)} %charge_hbm.1, f32[16,256]{1,0:T(8,128)} %bitcast.14, f32[16,32]{1,0:T(8,128)} %energy_hbm.1, f32[4096,1024]{1,0:T(8,128)} %factors_hbm.1, s32[16,1024]{1,0:T(8,128)} %bitcast.13, ...), custom_call_target="tpu_custom_call" | custom-call | tf_op jit(solution)/shard_map/pallas_call | solution.py:530
  48.0 1.4 %shard_map.166 = (f32[16,32]{1,0:T(8,128)}, f32[16,32]{1,0:T(8,128)}, f32[16,256]{1,0:T(8,128)}, f32[16,32]{1,0:T(8,128)}) custom-call(f32[16,32]{1,0:T(8,128)} %get-tuple-element.12.refs_0_, f32[16,32]{1,0:T(8,128)} %get-tuple-element.13.refs_1_, f32[16,256]{1,0:T(8,128)} %get-tuple-element.14.refs_2_, f32[16,32]{1,0:T(8,128)} %get-tuple-element.15.refs_3_), custom_call_target="tpu_custom_call" | custom-call | tf_op jit(solution)/shard_map/pallas_call | solution.py:571

commit v4 on v3

--- a/solution.py
+++ b/solution.py
@@ -132,6 +132,13 @@
     def peer(k):
         return lax.rem(chip + k, chips)
 
+    barrier = pltpu.get_barrier_semaphore()
+    for k in range(1, chips):
+        pl.semaphore_signal(
+            barrier, inc=1, device_id={"bus": 2 * peer(k) + core}, device_id_type=MESH
+        )
+    pl.semaphore_signal(barrier, inc=1, device_id={"bus": sibling}, device_id_type=MESH)
+
     dual_in = pltpu.make_async_copy(dual_hbm, dual_buf.at[0, chip], input_sem.at[0])
     fetches = [
         pltpu.make_async_copy(source, target, input_sem.at[1 + at])
@@ -167,27 +174,17 @@
     for fetch in fetches:
         fetch.start()
 
-    def load_factors(i, parity):
-        b = 2 * i + parity
+    def load_factors(slot):
+        own = lax.div(slot, chips)
+        b = 2 * lax.rem(slot, chips) + lax.rem(core + 1 + own, 2)
         start = pl.multiple_of(b * block, block)
         return pltpu.make_async_copy(
-            factors_hbm.at[pl.ds(start, block), :], factors_buf.at[b], factors_sem.at[b]
-        )
-
-    @pl.loop(0, chips)
-    def _(i):
-        load_factors(i, 1 - core).start()
-
-    @pl.loop(0, chips)
-    def _(i):
-        load_factors(i, core).start()
-
-    barrier = pltpu.get_barrier_semaphore()
-    for k in range(1, chips):
-        pl.semaphore_signal(
-            barrier, inc=1, device_id={"bus": 2 * peer(k) + core}, device_id_type=MESH
-        )
-    pl.semaphore_signal(barrier, inc=1, device_id={"bus": sibling}, device_id_type=MESH)
+            factors_hbm.at[pl.ds(start, block), :], factors_buf.at[slot], factors_sem.at[slot]
+        )
+
+    @pl.loop(0, n_bus)
+    def _(slot):
+        load_factors(slot).start()
 
     part_rows = hours // PARTS
 
@@ -210,6 +207,26 @@
             dst_ref=dual_buf.at[t, c, rows(part)],
             send_sem=dual_send_sem.at[t, part, 0],
             recv_sem=dual_recv_sem.at[t, part, c],
+            device_id={"bus": sibling},
+            device_id_type=MESH,
+        )
+
+    def send_first(k):
+        return pltpu.make_async_remote_copy(
+            src_ref=dual_buf.at[0, chip],
+            dst_ref=dual_buf.at[0, chip],
+            send_sem=dual_send_sem.at[0, 0, k],
+            recv_sem=dual_recv_sem.at[0, 0, chip],
+            device_id={"bus": 2 * peer(k) + core},
+            device_id_type=MESH,
+        )
+
+    def recv_first(c):
+        return pltpu.make_async_remote_copy(
+            src_ref=dual_buf.at[0, c],
+            dst_ref=dual_buf.at[0, c],
+            send_sem=dual_send_sem.at[0, 0, 0],
+            recv_sem=dual_recv_sem.at[0, 0, c],
             device_id={"bus": sibling},
             device_id_type=MESH,
         )
@@ -286,17 +303,21 @@
     pl.semaphore_wait(barrier, chips)
     dual_in.wait()
     for k in far_first:
-        for part in range(PARTS):
-            send_dual(0, k, part).start()
+        send_first(k).start()
     send_pack = to_sibling(pack_own, pack_sib, pack_sem)
     send_pack.start()
 
-    def take_columns(b, placed):
-        high, low = split_bf16(factors_buf[b])
-        place = place_buf[placed]
-        return jnp.dot(high, place, preferred_element_type=jnp.float32) + jnp.dot(
-            low, place, preferred_element_type=jnp.float32
-        )
+    together = 2 if chips % 2 == 0 else 1
+    taking = together * block
+
+    def take_columns(slot, placed):
+        high, low = split_bf16(factors_buf[pl.ds(slot, together)].reshape(taking, buses))
+        taken = jnp.dot(
+            jnp.concatenate([high, low], axis=0),
+            place_buf[placed],
+            preferred_element_type=jnp.float32,
+        )
+        return taken[:taking] + taken[taking:]
 
     def swap_columns(i):
         return pltpu.make_async_remote_copy(
@@ -308,30 +329,28 @@
             device_id_type=MESH,
         )
 
-    together = 2 if chips % 2 == 0 else 1
-
     @pl.loop(0, chips // together)
     def _(step):
         turns = [step * together + j for j in range(together)]
         for i in turns:
-            load_factors(i, 1 - core).wait()
-        for i in turns:
-            cols_send[i] = take_columns(2 * i + 1 - core, 1)
-        for i in turns:
+            load_factors(i).wait()
+        taken = take_columns(step * together, 1)
+        for j, i in enumerate(turns):
+            cols_send[i] = taken[j * block : (j + 1) * block]
             swap_columns(i).start()
 
     for k in reversed(far_first):
-        for part in range(PARTS):
-            recv_dual(0, peer(chips - k), part).wait_recv()
+        recv_first(peer(chips - k)).wait_recv()
 
     def collect(step, total):
         turns = [step * together + j for j in range(together)]
         for i in turns:
-            load_factors(i, core).wait()
+            load_factors(chips + i).wait()
         for i in turns:
             swap_columns(i).wait()
-        for i in turns:
-            mine = take_columns(2 * i + core, 0)
+        taken = take_columns(chips + step * together, 0)
+        for j, i in enumerate(turns):
+            mine = taken[j * block : (j + 1) * block]
             other = cols_recv[i]
             lane_at = lax.broadcasted_iota(jnp.int32, mine.shape, 1)
             columns = jnp.where(lane_at < half, mine, other)
@@ -349,6 +368,8 @@
     total = lax.fori_loop(
         0, chips // together, collect, jnp.zeros((2 * hours, 2 * width), jnp.float32)
     )
+    total = total[:hours] + total[hours:]
+    total = total[:, :width] + total[:, width:]
 
     send_pack.wait()
     state = pack_own[0] + pltpu.roll(pack_sib[0], half, 1)
@@ -373,31 +394,28 @@
             price_send.at[t, rows(part)], price_recv.at[t, rows(part)], price_sem.at[t, part]
         )
 
-    for t in range(ITERS):
-        partial = [None] * PARTS
-        for part in range(PARTS):
-            if t == 0:
-                both = total[:hours] + total[hours:]
-                both = both[rows(part)]
+    def partial_prices(t, own_dual, part):
+        total = jnp.zeros((2 * part_rows, 2 * width), jnp.float32)
+        for k in [0] + far_first[::-1]:
+            c = peer(chips - k)
+            if k == 0:
+                dual = own_dual
             else:
-                total = jnp.zeros((2 * part_rows, 2 * width), jnp.float32)
-                for k in [0] + far_first[::-1]:
-                    c = peer(chips - k)
-                    if k == 0:
-                        dual = own_dual[part]
-                    else:
-                        recv_dual(t, c, part).wait_recv()
-                        dual = dual_buf[t, c, rows(part)]
-                    total = total + jnp.dot(
-                        stacked(dual), turned_buf[c], preferred_element_type=jnp.float32
-                    )
-                both = total[:part_rows] + total[part_rows:]
-            partial[part] = both[:, :width] + both[:, width:]
-            price_send[t, rows(part)] = partial[part]
-            swap_prices(t, part).start()
-
-        bars = []
-        line_flows = []
+                recv_dual(t, c, part).wait_recv()
+                dual = dual_buf[t, c, rows(part)]
+            total = total + jnp.dot(
+                stacked(dual), turned_buf[c], preferred_element_type=jnp.float32
+            )
+        total = total[:part_rows] + total[part_rows:]
+        return total[:, :width] + total[:, width:]
+
+    def offer_prices(t, part, partial):
+        price_send[t, rows(part)] = partial
+        swap_prices(t, part).start()
+
+    def iterate(t, carry, last):
+        state, energy_dual, later, own_dual, partial = carry
+        new_state, bars, line_flows = [], [], []
         for part in range(PARTS):
             swap_prices(t, part).wait()
             prices = partial[part] + pltpu.roll(price_recv[t, rows(part)], half, 1)
@@ -405,7 +423,7 @@
             gradient = jnp.where(is_gen_part, cost + prices, pull - prices)
             step = jnp.clip(state[part] - primal_step * gradient, lower_part, upper)
             bar = 2.0 * step - state[part]
-            state[part] = step
+            new_state.append(step)
             bars.append(bar)
             pieces = stacked(jnp.where(is_gen_part, bar, -bar))
             pieces = jnp.concatenate([pieces, pieces], axis=1)
@@ -419,43 +437,66 @@
                 send_flow(t, k, part).start()
             line_flows.append(flows(chip))
 
-        if t + 1 == ITERS:
+        if last:
             for part in range(PARTS):
-                gen_out[rows(part)] = state[part][:, gens]
-                charge_out[rows(part)] = state[part][:, stors]
+                gen_out[rows(part)] = new_state[part][:, gens]
+                charge_out[rows(part)] = new_state[part][:, stors]
             stores[0].start()
             stores[1].start()
         so_far = running_sum(jnp.concatenate(bars, axis=0), False)
         energy = start_energy + efficiency * interval * so_far
         energy_dual = clip_dual(energy_dual + energy_step * energy, energy_step, 0.0, energy_limit)
-        if t + 1 < ITERS:
-            later = running_sum(energy_dual, True)
-        else:
+        if last:
             energy_out[...] = energy_dual[:, stors]
             stores[2].start()
-
+        else:
+            later = running_sum(energy_dual, True)
+
+        new_dual, new_partial = [], []
         for part in range(PARTS):
             flow = line_flows[part]
             for k in far_first[::-1]:
                 c = peer(chips - k)
                 recv_flow(t, c, part).wait_recv()
                 flow = flow + flow_recv[t, c, rows(part)]
-            own_dual[part] = clip_dual(
-                own_dual[part] + dual_step * flow, dual_step, -line_max, line_max
-            )
-            if t + 1 < ITERS:
-                dual_buf[t + 1, chip, rows(part)] = own_dual[part]
+            dual = clip_dual(own_dual[part] + dual_step * flow, dual_step, -line_max, line_max)
+            new_dual.append(dual)
+            if last:
+                dual_out[rows(part)] = dual
+            else:
+                dual_buf[t + 1, chip, rows(part)] = dual
                 for k in far_first:
                     send_dual(t + 1, k, part).start()
-            else:
-                dual_out[rows(part)] = own_dual[part]
-
-    stores[3].start()
-    for t in range(ITERS):
+        if last:
+            stores[3].start()
+        else:
+            for part in range(PARTS):
+                new_partial.append(partial_prices(t + 1, new_dual[part], part))
+                offer_prices(t + 1, part, new_partial[part])
+        return new_state, energy_dual, later, new_dual, new_partial
+
+    partial = [total[rows(part)] for part in range(PARTS)]
+    for part in range(PARTS):
+        offer_prices(0, part, partial[part])
+    carry = (state, energy_dual, later, own_dual, partial)
+    carry = lax.fori_loop(0, ITERS - 1, lambda t, carry: iterate(t, carry, False), carry)
+    iterate(ITERS - 1, carry, True)
+
+    for k in range(1, chips):
+        send_first(k).wait_send()
+
+    @pl.loop(0, ITERS)
+    def _(t):
+        for part in range(PARTS):
+            for k in range(1, chips):
+                send_flow(t, k, part).wait_send()
+
+    @pl.loop(1, ITERS)
+    def _(t):
         for part in range(PARTS):
             for k in range(1, chips):
                 send_dual(t, k, part).wait_send()
-                send_flow(t, k, part).wait_send()
+
     for store in stores:
         store.wait()
 

time: 49.6 us -> 49.2 us (level)
  no operation moved by 1% of the time
where the time goes in v4:
time: 49.2 us; the launch traced here: 49 us
  Pallas kernels  48.4 us (98%)
  between operations  0.64 us (1%)
    pallas_call x1, Pallas kernels, on_device_kernel(): pl.pallas_call(functools.partial(iterate_kernel, n_bus), out_shape=out_sh...  47 us
    pallas_call x1, Pallas kernels, on_device_kernel(): pl.pallas_call(store_kernel, out_shape=out_shape, in_specs=[hbm] * 4, out...  1.43 us

profile of v4, /device:TPU:0, one launch (start us, length us, event | category | flops | bytes accessed | tf_op | source)
XLA Modules:
  0.0 49.0 jit_solution(7943532571389064879)
XLA Ops:
  0.6 47.0 %shard_map.165 = (f32[16,32]{1,0:T(8,128)}, f32[16,32]{1,0:T(8,128)}, f32[16,256]{1,0:T(8,128)}, f32[16,32]{1,0:T(8,128)}) custom-call(f32[16,32]{1,0:T(8,128)} %bitcast.15, f32[16,32]{1,0:T(8,128)} %charge_hbm.1, f32[16,256]{1,0:T(8,128)} %bitcast.14, f32[16,32]{1,0:T(8,128)} %energy_hbm.1, f32[4096,1024]{1,0:T(8,128)} %factors_hbm.1, s32[16,1024]{1,0:T(8,128)} %bitcast.13, ...), custom_call_target="tpu_custom_call" | custom-call | tf_op jit(solution)/shard_map/pallas_call | solution.py:571
  47.6 1.4 %shard_map.166 = (f32[16,32]{1,0:T(8,128)}, f32[16,32]{1,0:T(8,128)}, f32[16,256]{1,0:T(8,128)}, f32[16,32]{1,0:T(8,128)}) custom-call(f32[16,32]{1,0:T(8,128)} %get-tuple-element.12.refs_0_, f32[16,32]{1,0:T(8,128)} %get-tuple-element.13.refs_1_, f32[16,256]{1,0:T(8,128)} %get-tuple-element.14.refs_2_, f32[16,32]{1,0:T(8,128)} %get-tuple-element.15.refs_3_), custom_call_target="tpu_custom_call" | custom-call | tf_op jit(solution)/shard_map/pallas_call | solution.py:612

commit v5 on v4

--- a/solution.py
+++ b/solution.py
@@ -102,6 +102,8 @@
     turned_buf,
     demand_buf,
     dual_buf,
+    across_send,
+    across_recv,
     flow_send,
     flow_recv,
     price_send,
@@ -111,10 +113,13 @@
     factors_sem,
     pack_sem,
     cols_sems,
+    first_sem,
     dual_send_sem,
     dual_recv_sem,
+    dual_across_sem,
     flow_send_sem,
     flow_recv_sem,
+    flow_across_sem,
     price_sem,
 ):
     chips = n_bus // 2
@@ -128,6 +133,17 @@
     chip = lax.div(me, 2)
     sibling = me + 1 - 2 * core
     far_first = sorted(range(1, chips), key=lambda k: abs(2 * k - chips))
+    depth = chips // 2
+    row = lax.rem(chip, 2)
+    place_z = lax.div(chip, 2)
+    across = 2 * (chip + 1 - 2 * row) + core
+    far_z = sorted(range(1, depth), key=lambda k: abs(2 * k - depth))
+
+    def peer_z(k):
+        return lax.rem(place_z + k, depth)
+
+    def device_z(k):
+        return 2 * (2 * peer_z(k) + row) + core
 
     def peer(k):
         return lax.rem(chip + k, chips)
@@ -139,7 +155,7 @@
         )
     pl.semaphore_signal(barrier, inc=1, device_id={"bus": sibling}, device_id_type=MESH)
 
-    dual_in = pltpu.make_async_copy(dual_hbm, dual_buf.at[0, chip], input_sem.at[0])
+    dual_in = pltpu.make_async_copy(dual_hbm, dual_buf.at[0, row, place_z], input_sem.at[0])
     fetches = [
         pltpu.make_async_copy(source, target, input_sem.at[1 + at])
         for at, (source, target) in enumerate(
@@ -191,64 +207,70 @@
     def rows(part):
         return slice(part * part_rows, (part + 1) * part_rows)
 
+    def remote(source, target, sent, received, device):
+        return pltpu.make_async_remote_copy(
+            src_ref=source,
+            dst_ref=target,
+            send_sem=sent,
+            recv_sem=received,
+            device_id={"bus": device},
+            device_id_type=MESH,
+        )
+
+    def send_first(k):
+        own = dual_buf.at[0, row, place_z]
+        return remote(
+            own, own, first_sem.at[0, k], first_sem.at[1, chip], 2 * peer(k) + core
+        )
+
+    def recv_first(c):
+        slot = dual_buf.at[0, lax.rem(c, 2), lax.div(c, 2)]
+        return remote(slot, slot, first_sem.at[0, 0], first_sem.at[1, c], sibling)
+
     def send_dual(t, k, part):
-        return pltpu.make_async_remote_copy(
-            src_ref=dual_buf.at[t, chip, rows(part)],
-            dst_ref=dual_buf.at[t, chip, rows(part)],
-            send_sem=dual_send_sem.at[t, part, k],
-            recv_sem=dual_recv_sem.at[t, part, chip],
-            device_id={"bus": 2 * peer(k) + core},
-            device_id_type=MESH,
-        )
-
-    def recv_dual(t, c, part):
-        return pltpu.make_async_remote_copy(
-            src_ref=dual_buf.at[t, c, rows(part)],
-            dst_ref=dual_buf.at[t, c, rows(part)],
-            send_sem=dual_send_sem.at[t, part, 0],
-            recv_sem=dual_recv_sem.at[t, part, c],
-            device_id={"bus": sibling},
-            device_id_type=MESH,
-        )
-
-    def send_first(k):
-        return pltpu.make_async_remote_copy(
-            src_ref=dual_buf.at[0, chip],
-            dst_ref=dual_buf.at[0, chip],
-            send_sem=dual_send_sem.at[0, 0, k],
-            recv_sem=dual_recv_sem.at[0, 0, chip],
-            device_id={"bus": 2 * peer(k) + core},
-            device_id_type=MESH,
-        )
-
-    def recv_first(c):
-        return pltpu.make_async_remote_copy(
-            src_ref=dual_buf.at[0, c],
-            dst_ref=dual_buf.at[0, c],
-            send_sem=dual_send_sem.at[0, 0, 0],
-            recv_sem=dual_recv_sem.at[0, 0, c],
-            device_id={"bus": sibling},
-            device_id_type=MESH,
+        own = dual_buf.at[t, row, place_z, rows(part)]
+        return remote(
+            own,
+            own,
+            dual_send_sem.at[t, part, k],
+            dual_recv_sem.at[t, part, place_z],
+            device_z(k),
+        )
+
+    def recv_dual(t, z, part):
+        slot = dual_buf.at[t, row, z, rows(part)]
+        return remote(
+            slot, slot, dual_send_sem.at[t, part, 0], dual_recv_sem.at[t, part, z], sibling
+        )
+
+    def pass_duals(t, part):
+        line = dual_buf.at[t, row, :, rows(part)]
+        return remote(
+            line, line, dual_across_sem.at[t, part, 0], dual_across_sem.at[t, part, 1], across
+        )
+
+    def pass_flows(t, part):
+        return remote(
+            across_send.at[t, :, rows(part)],
+            across_recv.at[t, :, rows(part)],
+            flow_across_sem.at[t, part, 0],
+            flow_across_sem.at[t, part, 1],
+            across,
         )
 
     def send_flow(t, k, part):
-        return pltpu.make_async_remote_copy(
-            src_ref=flow_send.at[t, k, rows(part)],
-            dst_ref=flow_recv.at[t, chip, rows(part)],
-            send_sem=flow_send_sem.at[t, part, k],
-            recv_sem=flow_recv_sem.at[t, part, chip],
-            device_id={"bus": 2 * peer(k) + core},
-            device_id_type=MESH,
-        )
-
-    def recv_flow(t, c, part):
-        return pltpu.make_async_remote_copy(
-            src_ref=flow_recv.at[t, c, rows(part)],
-            dst_ref=flow_recv.at[t, c, rows(part)],
-            send_sem=flow_send_sem.at[t, part, 0],
-            recv_sem=flow_recv_sem.at[t, part, c],
-            device_id={"bus": sibling},
-            device_id_type=MESH,
+        return remote(
+            flow_send.at[t, k, rows(part)],
+            flow_recv.at[t, place_z, rows(part)],
+            flow_send_sem.at[t, part, k],
+            flow_recv_sem.at[t, part, place_z],
+            device_z(k),
+        )
+
+    def recv_flow(t, z, part):
+        slot = flow_recv.at[t, z, rows(part)]
+        return remote(
+            slot, slot, flow_send_sem.at[t, part, 0], flow_recv_sem.at[t, part, z], sibling
         )
 
     def to_sibling(source, target, sems):
@@ -296,9 +318,9 @@
     first = me * units
     lane_start = pl.multiple_of(lax.div(first, LANES) * LANES, LANES)
     shift = lax.rem(units - lax.rem(first, LANES) + LANES, LANES)
-    for row, ref in ((1, charge_max_ref), (2, init_ref), (3, energy_max_ref)):
+    for param, ref in ((1, charge_max_ref), (2, init_ref), (3, energy_max_ref)):
         chunk = jnp.broadcast_to(ref[0:1, pl.ds(lane_start, LANES)], (8, LANES))
-        pack_own[2, row : row + 1, stors] = pltpu.roll(chunk, shift, 1)[0:1, stors]
+        pack_own[2, param : param + 1, stors] = pltpu.roll(chunk, shift, 1)[0:1, stors]
 
     pl.semaphore_wait(barrier, chips)
     dual_in.wait()
@@ -361,7 +383,8 @@
             weight_buf[i, width : 2 * width] = low
             demand = mine + pltpu.roll(other, half, 1)
             demand_buf[i] = load_unit * demand.T[half : half + hours]
-            pieces = jnp.concatenate(split_bf16(dual_buf[0, i]), axis=0)
+            first_dual = dual_buf[0, lax.rem(i, 2), lax.div(i, 2)]
+            pieces = jnp.concatenate(split_bf16(first_dual), axis=0)
             total = total + jnp.dot(pieces, turned, preferred_element_type=jnp.float32)
         return total
 
@@ -380,7 +403,7 @@
     is_gen = lax.rem(lane, half) < units
     lower = jnp.where(is_gen, 0.0, -upper)
     later = running_sum(energy_dual, True)
-    own_dual = [dual_buf[0, chip, rows(part)] for part in range(PARTS)]
+    own_dual = [dual_buf[0, row, place_z, rows(part)] for part in range(PARTS)]
     state = [state[rows(part)] for part in range(PARTS)]
     is_gen_part, lower_part = is_gen[:part_rows], lower[:part_rows]
     line_max = line_max_ref[...]
@@ -394,18 +417,10 @@
             price_send.at[t, rows(part)], price_recv.at[t, rows(part)], price_sem.at[t, part]
         )
 
-    def partial_prices(t, own_dual, part):
-        total = jnp.zeros((2 * part_rows, 2 * width), jnp.float32)
-        for k in [0] + far_first[::-1]:
-            c = peer(chips - k)
-            if k == 0:
-                dual = own_dual
-            else:
-                recv_dual(t, c, part).wait_recv()
-                dual = dual_buf[t, c, rows(part)]
-            total = total + jnp.dot(
-                stacked(dual), turned_buf[c], preferred_element_type=jnp.float32
-            )
+    def price_term(dual, c):
+        return jnp.dot(stacked(dual), turned_buf[c], preferred_element_type=jnp.float32)
+
+    def folded(total):
         total = total[:part_rows] + total[part_rows:]
         return total[:, :width] + total[:, width:]
 
@@ -432,10 +447,18 @@
                 out = jnp.dot(pieces, weight_buf[c], preferred_element_type=jnp.float32)
                 return out[:part_rows] + out[part_rows:] - demand_buf[c, rows(part)]
 
-            for k in far_first:
-                flow_send[t, k, rows(part)] = flows(peer(k))
+            for z in range(depth):
+                across_send[t, z, rows(part)] = flows(2 * z + 1 - row)
+            pass_flows(t, part).start()
+            line_flows.append({k: flows(2 * peer_z(k) + row) for k in far_z + [0]})
+
+        for part in range(PARTS):
+            pass_flows(t, part).wait_recv()
+            for k in far_z:
+                arrived = across_recv[t, peer_z(k), rows(part)]
+                flow_send[t, k, rows(part)] = line_flows[part][k] + arrived
                 send_flow(t, k, part).start()
-            line_flows.append(flows(chip))
+            line_flows[part] = line_flows[part][0] + across_recv[t, place_z, rows(part)]
 
         if last:
             for part in range(PARTS):
@@ -455,23 +478,38 @@
         new_dual, new_partial = [], []
         for part in range(PARTS):
             flow = line_flows[part]
-            for k in far_first[::-1]:
-                c = peer(chips - k)
-                recv_flow(t, c, part).wait_recv()
-                flow = flow + flow_recv[t, c, rows(part)]
+            for k in far_z[::-1]:
+                z = peer_z(depth - k)
+                recv_flow(t, z, part).wait_recv()
+                flow = flow + flow_recv[t, z, rows(part)]
             dual = clip_dual(own_dual[part] + dual_step * flow, dual_step, -line_max, line_max)
             new_dual.append(dual)
             if last:
                 dual_out[rows(part)] = dual
             else:
-                dual_buf[t + 1, chip, rows(part)] = dual
-                for k in far_first:
+                dual_buf[t + 1, row, place_z, rows(part)] = dual
+                for k in far_z:
                     send_dual(t + 1, k, part).start()
         if last:
             stores[3].start()
         else:
+            totals = []
             for part in range(PARTS):
-                new_partial.append(partial_prices(t + 1, new_dual[part], part))
+                for k in far_z[::-1]:
+                    recv_dual(t + 1, peer_z(depth - k), part).wait_recv()
+                pass_duals(t + 1, part).start()
+                total = jnp.zeros((2 * part_rows, 2 * width), jnp.float32)
+                for z in range(depth):
+                    dual = dual_buf[t + 1, row, z, rows(part)]
+                    total = total + price_term(dual, 2 * z + row)
+                totals.append(total)
+            for part in range(PARTS):
+                pass_duals(t + 1, part).wait_recv()
+                total = totals[part]
+                for z in range(depth):
+                    dual = dual_buf[t + 1, 1 - row, z, rows(part)]
+                    total = total + price_term(dual, 2 * z + 1 - row)
+                new_partial.append(folded(total))
                 offer_prices(t + 1, part, new_partial[part])
         return new_state, energy_dual, later, new_dual, new_partial
 
@@ -488,13 +526,15 @@
     @pl.loop(0, ITERS)
     def _(t):
         for part in range(PARTS):
-            for k in range(1, chips):
+            pass_flows(t, part).wait_send()
+            for k in range(1, depth):
                 send_flow(t, k, part).wait_send()
 
     @pl.loop(1, ITERS)
     def _(t):
         for part in range(PARTS):
-            for k in range(1, chips):
+            pass_duals(t, part).wait_send()
+            for k in range(1, depth):
                 send_dual(t, k, part).wait_send()
 
     for store in stores:
@@ -541,6 +581,7 @@
     block = flow_dual.shape[0]
     n_bus = lines // block
     chips = n_bus // 2
+    depth = chips // 2
     half = 2 * units
     width = 2 * half
     hbm = pl.BlockSpec(memory_space=pltpu.HBM)
@@ -589,9 +630,11 @@
             pltpu.VMEM((chips, 2 * width, block), jnp.bfloat16),
             pltpu.VMEM((chips, block, 2 * width), jnp.bfloat16),
             pltpu.VMEM((chips, hours, block), f32),
-            pltpu.VMEM((ITERS, chips, hours, block), f32),
-            pltpu.VMEM((ITERS, chips, hours, block), f32),
-            pltpu.VMEM((ITERS, chips, hours, block), f32),
+            pltpu.VMEM((ITERS, 2, depth, hours, block), f32),
+            pltpu.VMEM((ITERS, depth, hours, block), f32),
+            pltpu.VMEM((ITERS, depth, hours, block), f32),
+            pltpu.VMEM((ITERS, depth, hours, block), f32),
+            pltpu.VMEM((ITERS, depth, hours, block), f32),
             pltpu.VMEM((ITERS, hours, width), f32),
             pltpu.VMEM((ITERS, hours, width), f32),
             dma((len(arrays) - 1,)),
@@ -599,10 +642,13 @@
             dma((n_bus,)),
             dma((2,)),
             dma((2, chips)),
-            dma((ITERS, PARTS, chips)),
-            dma((ITERS, PARTS, chips)),
-            dma((ITERS, PARTS, chips)),
-            dma((ITERS, PARTS, chips)),
+            dma((2, chips)),
+            dma((ITERS, PARTS, depth)),
+            dma((ITERS, PARTS, depth)),
+            dma((ITERS, PARTS, 2)),
+            dma((ITERS, PARTS, depth)),
+            dma((ITERS, PARTS, depth)),
+            dma((ITERS, PARTS, 2)),
             dma((ITERS, PARTS, 2)),
         ],
         compiler_params=pltpu.CompilerParams(
@@ -683,7 +729,7 @@
     hours = charging.shape[0] // 2
     buses = shift_factors.shape[1] // n_bus
     return (
-        n_bus % 2 == 0
+        n_bus % 4 == 0
         and units == stors
         and 4 * units == LANES
         and hours == 16

time: 49.2 us -> 57.2 us (1.16)
  Pallas kernels: 48.4 us -> 56.4 us
    pallas_call x1, Pallas kernels: 47 us -> 55 us  [on_device_kernel(): pl.pallas_call(functools.partial(iterate_kernel, n_bus), out_shape=out_sh...]
where the time goes in v5:
time: 57.2 us; the launch traced here: 57 us
  Pallas kernels  56.4 us (99%)
  between operations  0.64 us (1%)
    pallas_call x1, Pallas kernels, on_device_kernel(): pl.pallas_call(functools.partial(iterate_kernel, n_bus), out_shape=out_sh...  55 us
    pallas_call x1, Pallas kernels, on_device_kernel(): pl.pallas_call(store_kernel, out_shape=out_shape, in_specs=[hbm] * 4, out...  1.43 us

profile of v5, /device:TPU:0, one launch (start us, length us, event | category | flops | bytes accessed | tf_op | source)
XLA Modules:
  0.0 57.0 jit_solution(9423707430523196028)
XLA Ops:
  0.6 55.0 %shard_map.165 = (f32[16,32]{1,0:T(8,128)}, f32[16,32]{1,0:T(8,128)}, f32[16,256]{1,0:T(8,128)}, f32[16,32]{1,0:T(8,128)}) custom-call(f32[16,32]{1,0:T(8,128)} %bitcast.15, f32[16,32]{1,0:T(8,128)} %charge_hbm.1, f32[16,256]{1,0:T(8,128)} %bitcast.14, f32[16,32]{1,0:T(8,128)} %energy_hbm.1, f32[4096,1024]{1,0:T(8,128)} %factors_hbm.1, s32[16,1024]{1,0:T(8,128)} %bitcast.13, ...), custom_call_target="tpu_custom_call" | custom-call | tf_op jit(solution)/shard_map/pallas_call | solution.py:612
  55.6 1.4 %shard_map.166 = (f32[16,32]{1,0:T(8,128)}, f32[16,32]{1,0:T(8,128)}, f32[16,256]{1,0:T(8,128)}, f32[16,32]{1,0:T(8,128)}) custom-call(f32[16,32]{1,0:T(8,128)} %get-tuple-element.12.refs_0_, f32[16,32]{1,0:T(8,128)} %get-tuple-element.13.refs_1_, f32[16,256]{1,0:T(8,128)} %get-tuple-element.14.refs_2_, f32[16,32]{1,0:T(8,128)} %get-tuple-element.15.refs_3_), custom_call_target="tpu_custom_call" | custom-call | tf_op jit(solution)/shard_map/pallas_call | solution.py:658

commit v6 on v4

--- a/solution.py
+++ b/solution.py
@@ -233,7 +233,7 @@
 
     def send_flow(t, k, part):
         return pltpu.make_async_remote_copy(
-            src_ref=flow_send.at[t, k, rows(part)],
+            src_ref=flow_send.at[t, peer(k), rows(part)],
             dst_ref=flow_recv.at[t, chip, rows(part)],
             send_sem=flow_send_sem.at[t, part, k],
             recv_sem=flow_recv_sem.at[t, part, chip],
@@ -357,8 +357,9 @@
             turned = jnp.concatenate(split_bf16(columns), axis=1)
             turned_buf[i] = turned
             high, low = split_bf16(columns.T)
-            weight_buf[i, 0:width] = high
-            weight_buf[i, width : 2 * width] = low
+            lines_at = pl.ds(pl.multiple_of(i * block, block), block)
+            weight_buf[0:width, lines_at] = high
+            weight_buf[width : 2 * width, lines_at] = low
             demand = mine + pltpu.roll(other, half, 1)
             demand_buf[i] = load_unit * demand.T[half : half + hours]
             pieces = jnp.concatenate(split_bf16(dual_buf[0, i]), axis=0)
@@ -394,18 +395,12 @@
             price_send.at[t, rows(part)], price_recv.at[t, rows(part)], price_sem.at[t, part]
         )
 
-    def partial_prices(t, own_dual, part):
-        total = jnp.zeros((2 * part_rows, 2 * width), jnp.float32)
-        for k in [0] + far_first[::-1]:
-            c = peer(chips - k)
-            if k == 0:
-                dual = own_dual
-            else:
-                recv_dual(t, c, part).wait_recv()
-                dual = dual_buf[t, c, rows(part)]
-            total = total + jnp.dot(
-                stacked(dual), turned_buf[c], preferred_element_type=jnp.float32
-            )
+    def partial_prices(t, part):
+        for k in far_first[::-1]:
+            recv_dual(t, peer(chips - k), part).wait_recv()
+        duals = jnp.concatenate([dual_buf[t, c, rows(part)] for c in range(chips)], axis=1)
+        turned = turned_buf[...].reshape(chips * block, 2 * width)
+        total = jnp.dot(stacked(duals), turned, preferred_element_type=jnp.float32)
         total = total[:part_rows] + total[part_rows:]
         return total[:, :width] + total[:, width:]
 
@@ -428,14 +423,14 @@
             pieces = stacked(jnp.where(is_gen_part, bar, -bar))
             pieces = jnp.concatenate([pieces, pieces], axis=1)
 
-            def flows(c):
-                out = jnp.dot(pieces, weight_buf[c], preferred_element_type=jnp.float32)
-                return out[:part_rows] + out[part_rows:] - demand_buf[c, rows(part)]
-
+            out = jnp.dot(pieces, weight_buf[...], preferred_element_type=jnp.float32)
+            out = out[:part_rows] + out[part_rows:]
+            for c in range(chips):
+                flow = out[:, c * block : (c + 1) * block] - demand_buf[c, rows(part)]
+                flow_send[t, c, rows(part)] = flow
             for k in far_first:
-                flow_send[t, k, rows(part)] = flows(peer(k))
                 send_flow(t, k, part).start()
-            line_flows.append(flows(chip))
+            line_flows.append(flow_send[t, chip, rows(part)])
 
         if last:
             for part in range(PARTS):
@@ -471,7 +466,7 @@
             stores[3].start()
         else:
             for part in range(PARTS):
-                new_partial.append(partial_prices(t + 1, new_dual[part], part))
+                new_partial.append(partial_prices(t + 1, part))
                 offer_prices(t + 1, part, new_partial[part])
         return new_state, energy_dual, later, new_dual, new_partial
 
@@ -586,7 +581,7 @@
             pltpu.VMEM((3, hours, width), f32),
             pltpu.VMEM((chips, block, LANES), f32),
             pltpu.VMEM((chips, block, LANES), f32),
-            pltpu.VMEM((chips, 2 * width, block), jnp.bfloat16),
+            pltpu.VMEM((2 * width, chips * block), jnp.bfloat16),
             pltpu.VMEM((chips, block, 2 * width), jnp.bfloat16),
             pltpu.VMEM((chips, hours, block), f32),
             pltpu.VMEM((ITERS, chips, hours, block), f32),

time: 49.2 us -> 48.9 us (level)
  no operation moved by 1% of the time
where the time goes in v6:
time: 48.9 us; the launch traced here: 48.7 us
  Pallas kernels  48.1 us (98%)
  between operations  0.64 us (1%)
    pallas_call x1, Pallas kernels, on_device_kernel(): pl.pallas_call(functools.partial(iterate_kernel, n_bus), out_shape=out_sh...  46.6 us
    pallas_call x1, Pallas kernels, on_device_kernel(): pl.pallas_call(store_kernel, out_shape=out_shape, in_specs=[hbm] * 4, out...  1.43 us

profile of v6, /device:TPU:0, one launch (start us, length us, event | category | flops | bytes accessed | tf_op | source)
XLA Modules:
  0.0 48.7 jit_solution(2127281872468569098)
XLA Ops:
  0.6 46.6 %shard_map.165 = (f32[16,32]{1,0:T(8,128)}, f32[16,32]{1,0:T(8,128)}, f32[16,256]{1,0:T(8,128)}, f32[16,32]{1,0:T(8,128)}) custom-call(f32[16,32]{1,0:T(8,128)} %bitcast.15, f32[16,32]{1,0:T(8,128)} %charge_hbm.1, f32[16,256]{1,0:T(8,128)} %bitcast.14, f32[16,32]{1,0:T(8,128)} %energy_hbm.1, f32[4096,1024]{1,0:T(8,128)} %factors_hbm.1, s32[16,1024]{1,0:T(8,128)} %bitcast.13, ...), custom_call_target="tpu_custom_call" | custom-call | tf_op jit(solution)/shard_map/pallas_call | solution.py:566
  47.3 1.4 %shard_map.166 = (f32[16,32]{1,0:T(8,128)}, f32[16,32]{1,0:T(8,128)}, f32[16,256]{1,0:T(8,128)}, f32[16,32]{1,0:T(8,128)}) custom-call(f32[16,32]{1,0:T(8,128)} %get-tuple-element.12.refs_0_, f32[16,32]{1,0:T(8,128)} %get-tuple-element.13.refs_1_, f32[16,256]{1,0:T(8,128)} %get-tuple-element.14.refs_2_, f32[16,32]{1,0:T(8,128)} %get-tuple-element.15.refs_3_), custom_call_target="tpu_custom_call" | custom-call | tf_op jit(solution)/shard_map/pallas_call | solution.py:607

commit v7 on v6

--- a/solution.py
+++ b/solution.py
@@ -9,7 +9,7 @@
 
 ITERS = 3
 LANES = 128
-PARTS = 2
+PARTS = 1
 VMEM_BYTES = 65472 * 1024
 MESH = pl.DeviceIdType.MESH
 

time: 48.9 us -> 50.6 us (1.035)
  Pallas kernels: 48.1 us -> 49.8 us
    pallas_call x1, Pallas kernels: 46.6 us -> 48.3 us  [on_device_kernel(): pl.pallas_call(functools.partial(iterate_kernel, n_bus), out_shape=out_sh...]
where the time goes in v7:
time: 50.6 us; the launch traced here: 50.4 us
  Pallas kernels  49.8 us (98%)
  between operations  0.64 us (1%)
    pallas_call x1, Pallas kernels, on_device_kernel(): pl.pallas_call(functools.partial(iterate_kernel, n_bus), out_shape=out_sh...  48.3 us
    pallas_call x1, Pallas kernels, on_device_kernel(): pl.pallas_call(store_kernel, out_shape=out_shape, in_specs=[hbm] * 4, out...  1.43 us

profile of v7, /device:TPU:0, one launch (start us, length us, event | category | flops | bytes accessed | tf_op | source)
XLA Modules:
  0.0 50.4 jit_solution(2162559638344131937)
XLA Ops:
  0.6 48.3 %shard_map.165 = (f32[16,32]{1,0:T(8,128)}, f32[16,32]{1,0:T(8,128)}, f32[16,256]{1,0:T(8,128)}, f32[16,32]{1,0:T(8,128)}) custom-call(f32[16,32]{1,0:T(8,128)} %bitcast.15, f32[16,32]{1,0:T(8,128)} %charge_hbm.1, f32[16,256]{1,0:T(8,128)} %bitcast.14, f32[16,32]{1,0:T(8,128)} %energy_hbm.1, f32[4096,1024]{1,0:T(8,128)} %factors_hbm.1, s32[16,1024]{1,0:T(8,128)} %bitcast.13, ...), custom_call_target="tpu_custom_call" | custom-call | tf_op jit(solution)/shard_map/pallas_call | solution.py:566
  49.0 1.4 %shard_map.166 = (f32[16,32]{1,0:T(8,128)}, f32[16,32]{1,0:T(8,128)}, f32[16,256]{1,0:T(8,128)}, f32[16,32]{1,0:T(8,128)}) custom-call(f32[16,32]{1,0:T(8,128)} %get-tuple-element.12.refs_0_, f32[16,32]{1,0:T(8,128)} %get-tuple-element.13.refs_1_, f32[16,256]{1,0:T(8,128)} %get-tuple-element.14.refs_2_, f32[16,32]{1,0:T(8,128)} %get-tuple-element.15.refs_3_), custom_call_target="tpu_custom_call" | custom-call | tf_op jit(solution)/shard_map/pallas_call | solution.py:607
